TPU v7x, 32 devices: a whole 2x2x4 slice. The times are simulated.
32 devices in a mesh: dp: 4 (over z), row: 2 (over core), col: 4 (over y, x).
Axes of the slice: x: 2, y: 2, z: 4, core: 2. Of those that a mesh axis runs over, the one named last changes fastest.
Arguments:
- tokens: bfloat16 [12608, 768], P(('dp', 'row'), 'col'), may hold values from -6 to 6
- cotangent: bfloat16 [12608, 768], P(('dp', 'row'), 'col'), may hold values from -6 to 6
- routes: int32 [12608, 2], P('dp'), may hold values from 0 to 31, all different within a row; in each aligned block of 3152 rows (0 to 3151, 3152 to 6303, ...) at most 400 rows name the same one
- adapter_pick: int32 [64], replicated, may hold values from 0 to 7
- gain_attn: float32 [768], P('col'), may hold values from 0.5 to 1.5
- gain_moe: float32 [768], P('col'), may hold values from 0.5 to 1.5
- w_qkv: bfloat16 [3, 768, 768], P(None, 'col', 'row'), may hold values from -0.21875 to 0.21875
- w_out: bfloat16 [768, 768], P('row', 'col'), may hold values from -0.875 to 0.875
- w_router: bfloat16 [768, 32], replicated, may hold values from -0.15625 to 0.15625
- w_up: bfloat16 [32, 768, 3072], P(None, None, ('row', 'col')), may hold values from -0.21875 to 0.21875
- w_down: bfloat16 [32, 3072, 768], P(None, ('row', 'col')), may hold values from -1.75 to 1.75
- a_qkv: bfloat16 [3, 768, 128], P(None, 'col'), may hold values from -0.21875 to 0.21875
- b_qkv: bfloat16 [3, 128, 768], P(None, None, 'row'), may hold values from -0.75 to 0.75
- a_out: bfloat16 [768, 128], P('row'), may hold values from -0.875 to 0.875
- b_out: bfloat16 [128, 768], P(None, 'col'), may hold values from -0.75 to 0.75
- a_router: bfloat16 [768, 128], replicated, may hold values from -0.21875 to 0.21875
- b_router: bfloat16 [128, 32], replicated, may hold values from -0.5 to 0.5
- a_up: bfloat16 [768, 128], replicated, may hold values from -0.21875 to 0.21875
- b_up: bfloat16 [128, 3072], P(None, ('row', 'col')), may hold values from -0.75 to 0.75
- a_down: bfloat16 [3072, 128], P(('row', 'col')), may hold values from -0.109375 to 0.109375
- b_down: bfloat16 [128, 768], replicated, may hold values from -1.5 to 1.5
Outputs:
- block_out: bfloat16 [12608, 768], P(('dp', 'row'), 'col')
- grad_tokens: float32 [12608, 768], P(('dp', 'row'), 'col')
- grad_a_qkv: float32 [3, 768, 128], P(None, 'col')
- grad_b_qkv: float32 [3, 128, 768], P(None, None, 'row')
- grad_a_out: float32 [768, 128], P('row')
- grad_b_out: float32 [128, 768], P(None, 'col')
- grad_a_router: float32 [768, 128], replicated
- grad_b_router: float32 [128, 32], replicated
- grad_a_up: float32 [768, 128], replicated
- grad_b_up: float32 [128, 3072], P(None, ('row', 'col'))
- grad_a_down: float32 [3072, 128], P(('row', 'col'))
- grad_b_down: float32 [128, 768], replicated
Inputs may be any that keep to these rules, and one draw needn't show every extreme that they name: `routes`: each token names two different experts. In each aligned block of 3152 rows (the tokens of one index of dp) no expert is named by more than 400 rows, and in some block one expert is named by exactly 400 rows.
All inputs are finite; a program needn't handle non-finite values.
Results may differ from a plain program's by a relative error of at most 0.035.
Values may be sent and summed in bfloat16 or wider, within the bound.
No kernel may reach another device: no remote copies, remote signals or barrier semaphores. Data moves between devices by JAX's collectives and lax.ppermute only.
A program may use at most 448 MiB of HBM per device.

v0:
```python
import jax
import jax.numpy as jnp
from jax import lax
from jax.sharding import PartitionSpec as P

D = 768
HEAD_DIM = 64
EXPERTS = 32
SEQ = 197
RANK = 16
ADAPTERS = 8
IMG_GRP = 16
CAP = 400


highest = lax.Precision.HIGHEST
epsilon = 1e-06


def as_sent(value):
    return jax.tree.map(lambda a: a.astype(jnp.bfloat16) if a.dtype == jnp.float32 else a, value)


def matmul(left, right):
    return jnp.dot(left, right, preferred_element_type=jnp.float32)


def precise(left, right):
    return jnp.dot(left, right, precision=highest, preferred_element_type=jnp.float32)


def split_dot(left, right):
    if left.dtype == jnp.float32:
        leading = left.astype(jnp.bfloat16)
        trailing = (left - leading.astype(jnp.float32)).astype(jnp.bfloat16)
        return matmul(leading, right) + matmul(trailing, right)
    leading = right.astype(jnp.bfloat16)
    trailing = (right - leading.astype(jnp.float32)).astype(jnp.bfloat16)
    return matmul(left, leading) + matmul(left, trailing)


def adapter_mask(adapter_pick, first, count):
    chosen = lax.dynamic_slice_in_dim(adapter_pick, first, count)
    per_token = jnp.repeat(chosen, SEQ)
    columns = jnp.arange(ADAPTERS * RANK, dtype=jnp.int32) // RANK
    return (columns[None, :] == per_token[:, None]).astype(jnp.float32)


def expert_slots(routes_in):
    flattened = routes_in.reshape(-1)
    onehot = (flattened[:, None] == jnp.arange(EXPERTS, dtype=jnp.int32)[None, :]).astype(jnp.int32)
    earlier = jnp.cumsum(onehot, axis=0) - onehot
    position = jnp.sum(earlier * onehot, axis=1)
    slot_of = flattened * CAP + position
    counter = jnp.arange(flattened.shape[0], dtype=jnp.int32) + 1
    source = jnp.zeros((EXPERTS * CAP,), jnp.int32).at[slot_of].set(counter)
    return (slot_of.reshape(-1, 2), source)


def feature_sums(first, second):
    return lax.psum((jnp.sum(first, axis=1), jnp.sum(second, axis=1)), "col")


def norm_forward(rows_in, gain_vec):
    total, square = feature_sums(rows_in, rows_in * rows_in)
    centre = total[:, None] / D
    spread = square[:, None] / D - centre * centre
    inverse = lax.rsqrt(spread + epsilon)
    unit_rows = (rows_in - centre) * inverse
    return (unit_rows * gain_vec, unit_rows, inverse)


def norm_backward(grad_in, gain_vec, unit_rows, inverse):
    scaled = grad_in * gain_vec
    total, along = feature_sums(scaled, scaled * unit_rows)
    return inverse * (scaled - total[:, None] / D - unit_rows * along[:, None] / D)


def group_rows(parts):
    return jax.tree.map(
        lambda part, own: part.astype(own.dtype),
        lax.all_gather(as_sent(parts), "row", axis=0, tiled=True),
        parts,
    )


def sum_rows(partial_value):
    return lax.psum_scatter(
        partial_value.astype(jnp.bfloat16), "row", scatter_dimension=0, tiled=True
    ).astype(jnp.float32)


def col_rows(values_in):
    return lax.all_gather(values_in, "col", axis=0, tiled=True)


def col_parts(term_fn, rows_out):
    return lax.psum_scatter(
        term_fn(jnp.int32(0), rows_out * lax.axis_size("col")).astype(jnp.bfloat16),
        "col",
        scatter_dimension=0,
        tiled=True,
    ).astype(jnp.float32)


def whole_features(parts):
    return jax.tree.map(
        lambda part, own: part.astype(own.dtype),
        lax.all_gather(as_sent(parts), "col", axis=1, tiled=True),
        parts,
    )


def fold_tokens(partial_value):
    return lax.psum_scatter(
        sum_rows(partial_value).astype(jnp.bfloat16), "col", scatter_dimension=1, tiled=True
    ).astype(jnp.float32)


def on_device(
    tokens,
    cotangent,
    routes,
    adapter_pick,
    gain_attn,
    gain_moe,
    w_qkv,
    w_out,
    w_router,
    w_up,
    w_down,
    a_qkv,
    b_qkv,
    a_out,
    b_out,
    a_router,
    b_router,
    a_up,
    b_up,
    a_down,
    b_down,
):
    n_row = lax.axis_size("row")
    n_col = lax.axis_size("col")
    row_idx = lax.axis_index("row")
    col_idx = lax.axis_index("col")
    group_first = lax.axis_index("dp") * IMG_GRP
    rows_here = tokens.shape[0]
    cols_here = tokens.shape[1]
    rows_group = rows_here * n_row
    rows_cols = rows_group // n_col
    half_feat = w_qkv.shape[2]
    images_cols = IMG_GRP // n_col
    heads_here = half_feat // HEAD_DIM
    factor = HEAD_DIM ** (-0.5)
    mask_group = adapter_mask(adapter_pick, group_first, IMG_GRP)
    resid = tokens.astype(jnp.float32)
    normed_f, unit_one, scale_one = norm_forward(resid, gain_attn)
    normed = normed_f.astype(jnp.bfloat16)
    normed_group = group_rows((normed,))[0]
    low_qkv = [matmul(normed_group, a_qkv[member]) for member in range(3)]
    w_joined = jnp.concatenate([w_qkv[0], w_qkv[1], w_qkv[2]], axis=1)

    def qkv_term(start, count):
        extra = [split_dot(low_qkv[member] * mask_group, b_qkv[member]) for member in range(3)]
        return matmul(normed_group, w_joined) + jnp.concatenate(extra, axis=1)

    qkv_pre = col_parts(qkv_term, rows_cols)
    shaped = qkv_pre.astype(jnp.bfloat16).reshape(images_cols, SEQ, 3, heads_here, HEAD_DIM)
    queries = shaped[:, :, 0]
    keys_in = shaped[:, :, 1]
    values_in = shaped[:, :, 2]
    scores = (
        jnp.einsum("iqhd,ikhd->ihqk", queries, keys_in, preferred_element_type=jnp.float32) * factor
    )
    highest_score = jnp.max(scores, axis=-1, keepdims=True)
    log_total = highest_score + jnp.log(
        jnp.sum(jnp.exp(scores - highest_score), axis=-1, keepdims=True)
    )
    weights = jnp.exp(scores - log_total).astype(jnp.bfloat16)
    mixed = jnp.einsum("ihqk,ikhd->iqhd", weights, values_in, preferred_element_type=jnp.float32)
    mixed = mixed.reshape(rows_cols, half_feat).astype(jnp.bfloat16)
    mixed_group = col_rows(mixed)
    low_out = matmul(mixed_group, a_out)
    attention = sum_rows(matmul(mixed_group, w_out) + split_dot(low_out * mask_group, b_out))
    resid_two = resid + attention
    normed_two_f, unit_two, scale_two = norm_forward(resid_two, gain_moe)
    normed_two = normed_two_f.astype(jnp.bfloat16)
    full_two, full_cot = group_rows(whole_features((normed_two, cotangent)))
    low_router = matmul(full_two, a_router)
    logits = matmul(full_two, w_router) + split_dot(low_router * mask_group, b_router)
    router_probs = jax.nn.softmax(logits, axis=-1)
    gate_vals = jnp.take_along_axis(router_probs, routes, axis=1)
    slot_of, source = expert_slots(routes)
    token_src = jnp.where(source > 0, (source - 1) // 2 + 1, 0)
    padded_two = jnp.concatenate([jnp.zeros((1, D), jnp.bfloat16), full_two], axis=0)
    inputs = jnp.take(padded_two, token_src, axis=0).reshape(EXPERTS, CAP, D)
    slot_mask = jnp.take(
        jnp.concatenate([jnp.zeros((1, ADAPTERS * RANK), jnp.float32), mask_group], axis=0),
        token_src,
        axis=0,
    )
    low_up = jnp.concatenate(
        [jnp.zeros((1, ADAPTERS * RANK), jnp.float32), matmul(full_two, a_up)], axis=0
    )
    slot_low = jnp.take(low_up, token_src, axis=0) * slot_mask
    dense = jnp.einsum("ecd,edf->ecf", inputs, w_up, preferred_element_type=jnp.float32)
    hidden = dense + split_dot(slot_low, b_up).reshape(EXPERTS, CAP, -1)
    activated = jax.nn.gelu(hidden, approximate=False).astype(jnp.bfloat16)
    flat_act = activated.reshape(EXPERTS * CAP, -1)
    low_down = matmul(flat_act, a_down) * slot_mask
    expert_out = jnp.einsum(
        "ecf,efd->ecd", activated, w_down, preferred_element_type=jnp.float32
    ).reshape(EXPERTS * CAP, D)
    expert_out = expert_out + split_dot(low_down, b_down)
    first_pick = jnp.take(expert_out, slot_of[:, 0], axis=0)
    second_pick = jnp.take(expert_out, slot_of[:, 1], axis=0)
    expert_part = gate_vals[:, 0:1] * first_pick + gate_vals[:, 1:2] * second_pick
    cot_group = full_cot.astype(jnp.float32)
    gate_part = jnp.stack(
        [jnp.sum(cot_group * first_pick, axis=1), jnp.sum(cot_group * second_pick, axis=1)], axis=1
    )
    expert_sum = fold_tokens(expert_part)
    block_out = (resid_two + expert_sum).astype(jnp.bfloat16)
    grad_gates = lax.psum(gate_part, ("row", "col"))
    gate_src = jnp.take(
        jnp.concatenate([jnp.zeros((1,), jnp.float32), gate_vals.reshape(-1)]), source, axis=0
    )
    padded_cot = jnp.concatenate([jnp.zeros((1, D), jnp.bfloat16), full_cot], axis=0)
    grad_back = (
        jnp.take(padded_cot, token_src, axis=0).astype(jnp.float32) * gate_src[:, None]
    ).astype(jnp.bfloat16)
    grad_low_down = matmul(grad_back, b_down.T) * slot_mask
    grad_act = jnp.einsum(
        "ecd,efd->ecf",
        grad_back.reshape(EXPERTS, CAP, D),
        w_down,
        preferred_element_type=jnp.float32,
    )
    grad_act = grad_act + split_dot(grad_low_down, a_down.T).reshape(EXPERTS, CAP, -1)
    part_a_down = split_dot(flat_act.T, grad_low_down)
    part_b_down = split_dot(low_down.T, grad_back)
    unused, gelu_back = jax.vjp(lambda value_in: jax.nn.gelu(value_in, approximate=False), hidden)
    grad_hidden = gelu_back(grad_act)[0].astype(jnp.bfloat16)
    flat_grad = grad_hidden.reshape(EXPERTS * CAP, -1)
    grad_inputs = jnp.einsum(
        "ecf,edf->ecd", grad_hidden, w_up, preferred_element_type=jnp.float32
    ).reshape(EXPERTS * CAP, D)
    grad_low_up = matmul(flat_grad, b_up.T)
    part_b_up = split_dot(slot_low.T, flat_grad)
    token_grad = jnp.take(grad_inputs, slot_of[:, 0], axis=0) + jnp.take(
        grad_inputs, slot_of[:, 1], axis=0
    )
    token_low = (
        jnp.take(grad_low_up, slot_of[:, 0], axis=0) + jnp.take(grad_low_up, slot_of[:, 1], axis=0)
    ) * mask_group
    token_grad = token_grad + split_dot(token_low, a_up.T)
    part_a_up = split_dot(full_two.T, token_low)
    expert_ids = jnp.arange(EXPERTS, dtype=jnp.int32)
    grad_probs = jnp.sum(
        (routes[:, :, None] == expert_ids[None, None, :]).astype(jnp.float32)
        * grad_gates[:, :, None],
        axis=1,
    )
    grad_logits = router_probs * (
        grad_probs - jnp.sum(router_probs * grad_probs, axis=-1, keepdims=True)
    )
    grad_low_router = split_dot(grad_logits, b_router.T) * mask_group
    router_back = split_dot(grad_logits, w_router.T) + split_dot(grad_low_router, a_router.T)
    part_a_router = split_dot(full_two.T, grad_low_router)
    part_b_router = precise((low_router * mask_group).T, grad_logits)
    grad_two = fold_tokens(token_grad)
    grad_two = grad_two + lax.dynamic_slice(
        router_back, (row_idx * rows_here, col_idx * cols_here), (rows_here, cols_here)
    )
    grad_resid = cotangent.astype(jnp.float32) + norm_backward(
        grad_two, gain_moe, unit_two, scale_two
    )
    grad_attn = grad_resid.astype(jnp.bfloat16)
    grad_attn_group = group_rows((grad_attn,))[0]
    grad_low_out = matmul(grad_attn_group, b_out.T) * mask_group

    def mixed_term(start, count):
        return matmul(grad_attn_group, w_out.T) + split_dot(grad_low_out, a_out.T)

    grad_mixed = col_parts(mixed_term, rows_cols).astype(jnp.bfloat16)
    part_a_out = split_dot(mixed_group.T, grad_low_out)
    part_b_out = split_dot((low_out * mask_group).T, grad_attn_group)
    grad_shaped = grad_mixed.reshape(images_cols, SEQ, heads_here, HEAD_DIM)
    scores_again = (
        jnp.einsum("iqhd,ikhd->ihqk", queries, keys_in, preferred_element_type=jnp.float32) * factor
    )
    probs_again = jnp.exp(scores_again - log_total)
    grad_weights = jnp.einsum(
        "iqhd,ikhd->ihqk", grad_shaped, values_in, preferred_element_type=jnp.float32
    )
    grad_scores = (
        probs_again * (grad_weights - jnp.sum(probs_again * grad_weights, axis=-1, keepdims=True))
    ).astype(jnp.bfloat16)
    grad_queries = (
        jnp.einsum("ihqk,ikhd->iqhd", grad_scores, keys_in, preferred_element_type=jnp.float32)
        * factor
    )
    grad_keys = (
        jnp.einsum("ihqk,iqhd->ikhd", grad_scores, queries, preferred_element_type=jnp.float32)
        * factor
    )
    grad_values = jnp.einsum(
        "ihqk,iqhd->ikhd",
        probs_again.astype(jnp.bfloat16),
        grad_shaped,
        preferred_element_type=jnp.float32,
    )
    grad_qkv = (
        jnp.stack([grad_queries, grad_keys, grad_values], axis=2)
        .reshape(rows_cols, 3 * half_feat)
        .astype(jnp.bfloat16)
    )
    grad_group = col_rows(grad_qkv)
    grad_normed_part = jnp.zeros((rows_group, cols_here), jnp.float32)
    a_parts = []
    b_parts = []
    for member in range(3):
        piece = grad_group[:, member * half_feat : (member + 1) * half_feat]
        grad_low = matmul(piece, b_qkv[member].T) * mask_group
        grad_normed_part = (
            grad_normed_part + matmul(piece, w_qkv[member].T) + split_dot(grad_low, a_qkv[member].T)
        )
        a_parts.append(split_dot(normed_group.T, grad_low))
        b_parts.append(split_dot((low_qkv[member] * mask_group).T, piece))
    grad_normed = sum_rows(grad_normed_part)
    grad_tokens = grad_resid + norm_backward(grad_normed, gain_attn, unit_one, scale_one)
    col_total = lax.psum((jnp.stack(b_parts), part_a_out), ("dp", "col"))
    row_total = lax.psum((jnp.stack(a_parts), part_b_out), ("dp", "row"))
    dp_total = (
        lax.psum(part_a_router.astype(jnp.bfloat16), "dp").astype(jnp.float32),
        lax.psum(part_b_router.astype(jnp.bfloat16), "dp").astype(jnp.float32),
        lax.psum(part_b_up.astype(jnp.bfloat16), "dp").astype(jnp.float32),
        lax.psum(part_a_down.astype(jnp.bfloat16), "dp").astype(jnp.float32),
    )
    all_total = lax.psum((part_a_up, part_b_down), ("dp", "row", "col"))
    return (
        block_out,
        grad_tokens,
        row_total[0],
        col_total[0],
        col_total[1],
        row_total[1],
        dp_total[0],
        dp_total[1],
        all_total[0],
        dp_total[2],
        dp_total[3],
        all_total[1],
    )


def solution(mesh):
    return jax.shard_map(
        on_device,
        mesh=mesh,
        in_specs=(
            P(("dp", "row"), "col"),
            P(("dp", "row"), "col"),
            P("dp", None),
            P(),
            P("col"),
            P("col"),
            P(None, "col", "row"),
            P("row", "col"),
            P(),
            P(None, None, ("row", "col")),
            P(None, ("row", "col"), None),
            P(None, "col", None),
            P(None, None, "row"),
            P("row", None),
            P(None, "col"),
            P(),
            P(),
            P(),
            P(None, ("row", "col")),
            P(("row", "col"), None),
            P(),
        ),
        out_specs=(
            P(("dp", "row"), "col"),
            P(("dp", "row"), "col"),
            P(None, "col", None),
            P(None, None, "row"),
            P("row", None),
            P(None, "col"),
            P(),
            P(),
            P(),
            P(None, ("row", "col")),
            P(("row", "col"), None),
            P(),
        ),
        check_vma=False,
    )
```

profile of v0, /device:TPU:0, one launch (start us, length us, event | category | flops | bytes accessed | tf_op | source)
XLA Modules:
  0.0 1925.9 jit_solution(17976972037981973316)
XLA Ops:
  8.6 17.5 all-reduce.15
  64.8 84.6 %fusion = bf16[800,1152]{1,0:T(8,128)(2,1)S(1)} fusion(bf16[3152,1152]{1,0:T(8,128)(2,1)} %fusion.8), kind=kCustom, calls=%all-reduce-scatter | all-reduce-scatter fusion | flops 3686401 | bytes 9105920
  190.9 39.6 %all-gather.23.cloned.1.call-done = bf16[4,788,384]{2,1,0:T(8,128)(2,1)} async-done(((bf16[1,788,384]{2,1,0:T(8,128)(2,1)}), bf16[4,788,384]{2,1,0:T(8,128)(2,1)}) %all-gather.23.cloned.1.call-update) | async-done | bytes 2420752 | tf_op jit(solution)/shard_map/all_gather | solution.py:94
  268.2 22.6 %all-gather.17.cloned.1.call-done = bf16[1576,768]{0,1:T(8,128)(2,1)} async-done(((bf16[1576,192]{0,1:T(8,128)(2,1)}), bf16[1576,768]{0,1:T(8,128)(2,1)}) %all-gather.17.cloned.1.call-update) | async-done | bytes 2420752 | tf_op jit(solution)/shard_map/all_gather | solution.py:109
  298.0 16.9 reduce-window.6
  344.6 30.1 %scatter_custom_fusion = s32[12800]{0:T(1024)S(1)} fusion(s32[6304]{0:T(1024)S(1)} %fusion.246, s32[6304]{0:T(1024)S(1)} %iota_add_fusion, s32[]{:T(128)} %constant.99.clone.1), kind=kCustom, calls=%fused_computation.383 | custom fusion | bytes 51204 | tf_op jit(solution)/shard_map/scatter | solution.py:56
  377.0 24.1 %gather_fusion.4 = f32[12800,128]{1,0:T(8,128)} fusion(f32[3153,128]{1,0:T(8,128)S(1)} %pad_convert_fusion, s32[13312]{0:T(1024)S(1)} %pad_clamp_fusion.1), kind=kCustom, calls=%fused_computation.5.clone | custom fusion | bytes 13158400 | tf_op jit(solution)/shard_map/jit(_take)/gather | solution.py:198
  410.8 49.4 %gather_fusion.7 = bf16[12800,768]{1,0:T(8,128)(2,1)} fusion(bf16[3153,768]{1,0:T(8,128)(2,1)} %concatenate.29, s32[13312]{0:T(1024)S(1)} %pad_clamp_fusion.1), kind=kCustom, calls=%fused_computation.4.clone | custom fusion | bytes 39372800 | tf_op jit(solution)/shard_map/jit(_take)/gather | solution.py:231
  469.9 49.4 %gather_fusion.2 = bf16[12800,768]{1,0:T(8,128)(2,1)} fusion(bf16[3153,768]{1,0:T(8,128)(2,1)} %concatenate.25, s32[13312]{0:T(1024)S(1)} %pad_clamp_fusion.1), kind=kCustom, calls=%fused_computation.clone | custom fusion | bytes 39372800 | tf_op jit(solution)/shard_map/jit(_take)/gather | solution.py:197
  523.2 24.2 %gather_fusion.3 = f32[12800,128]{1,0:T(8,128)} fusion(f32[3153,128]{1,0:T(8,128)S(1)} %concatenate.26, s32[13312]{0:T(1024)S(1)} %pad_clamp_fusion.1), kind=kCustom, calls=%fused_computation.1.clone | custom fusion | bytes 13158400 | tf_op jit(solution)/shard_map/jit(_take)/gather | solution.py:206
  547.5 19.1 broadcast_select_fusion
  587.2 19.7 %convolution_add_fusion.2 = f32[12800,384]{1,0:T(8,128)} fusion(f32[12800,384]{1,0:T(8,128)} %fusion.37, bf16[128,384]{1,0:T(8,128)(2,1)S(1)} %copy-done.68, f32[12800,128]{1,0:T(8,128)} %copy-done.6), kind=kOutput, calls=%fused_computation.39 | convolution fusion | flops 1269760000 | bytes 45973504 | tf_op jit(solution)/shard_map/dot_general | solution.py:25
  606.9 31.4 %convert_reduce_fusion.1 = (u32[400,384]{1,0:T(8,128)S(1)}, u32[400,384]{1,0:T(8,128)S(1)}, f32[32,400,384]{2,1,0:T(8,128)}) fusion(f32[32,400,384]{2,1,0:T(8,128)} %bitcast.317, bf16[32,400,768]{2,1,0:T(8,128)(2,1)} %bitcast.319, bf16[32,768,384]{2,1,0:T(8,128)(2,1)} %param.38), kind=kOutput, calls=%fused_computation.21 | convolution fusion | flops 7608422400 | bytes 79085568 | tf_op jit(solution)/shard_map/ecd,edf->ecf/dot_general | solution.py:207
  638.3 46.3 %multiply_convert_fusion.1 = (bf16[32,400,384]{2,1,0:T(8,128)(2,1)}, f32[32,400,384]{2,1,0:T(8,128)}) fusion(f32[32,400,384]{2,1,0:T(8,128)} %get-tuple-element.72, u32[400,384]{1,0:T(8,128)S(1)} %get-tuple-element.17, u32[400,384]{1,0:T(8,128)S(1)} %get-tuple-element.16), kind=kLoop, calls=%fused_computation.23 | loop fusion | flops 334233600 | bytes 50380800 | tf_op jit(solution)/shard_map/convert_element_type | solution.py:209
  684.6 25.3 %fusion.313 = f32[32,400,768]{2,1,0:T(8,128)} fusion(bf16[32,400,384]{2,1,0:T(8,128)(2,1)} %get-tuple-element.52, bf16[32,384,768]{2,1,0:T(8,128)(2,1)} %param.39), kind=kOutput, calls=%fused_computation.465 | convolution fusion | flops 7549747200 | bytes 68026368 | tf_op jit(solution)/shard_map/ecf,efd->ecd/dot_general | solution.py:212
  737.6 46.0 %bitcast_add_fusion = f32[12800,768]{1,0:T(8,128)} fusion(f32[32,400,768]{2,1,0:T(8,128)} %fusion.313, f32[12800,768]{1,0:T(8,128)} %fusion.34, bf16[128,768]{1,0:T(8,128)(2,1)S(1)} %copy-done, f32[12800,128]{1,0:T(8,128)} %copy-done.8), kind=kOutput, calls=%fused_computation.13 | convolution fusion | flops 2542796800 | bytes 124715008 | tf_op jit(solution)/shard_map/dot_general | solution.py:25
  783.6 25.2 %gather_fusion.6 = f32[3152,768]{1,0:T(8,128)} fusion(f32[12800,768]{1,0:T(8,128)} %bitcast_add_fusion, s32[4096]{0:T(1024)S(1)} %copy-done.89), kind=kCustom, calls=%fused_computation.6.clone | custom fusion | bytes 19378496 | tf_op jit(solution)/shard_map/jit(_take)/gather | solution.py:217
  808.8 25.2 %gather_fusion.5 = f32[3152,768]{1,0:T(8,128)} fusion(f32[12800,768]{1,0:T(8,128)} %bitcast_add_fusion, s32[4096]{0:T(1024)S(1)} %copy-done.91), kind=kCustom, calls=%fused_computation.2.clone | custom fusion | bytes 19378496 | tf_op jit(solution)/shard_map/jit(_take)/gather | solution.py:216
  844.3 26.8 %psum.137 = f32[3152,2]{0,1:T(2,128)S(1)} all-reduce(f32[3152,2]{0,1:T(2,128)S(1)} %pad_maximum_fusion.4), channel_id=1, replica_groups=mesh['dp'=4,'row'=2,'col'=4] {'row','col'}, use_global_device_ids=true, to_apply=%region_24.29 | all-reduce | flops 6304 | bytes 50432 | tf_op jit(solution)/shard_map/psum | solution.py:225
  876.1 48.4 %gather_fusion.1 = f32[6304]{0:T(1024)S(1)} fusion(f32[3152,32]{0,1:T(8,128)S(1)} %get-tuple-element.51, s32[6304]{0:T(1024)S(1)} %copy-done.4), kind=kCustom, calls=%fused_computation.11 | custom fusion | bytes 100864 | tf_op jit(solution)/shard_map/jit(take_along_axis)/gather | solution.py:193
  928.2 65.9 %gather_fusion = f32[12800]{0:T(1024)S(1)} fusion(f32[6305]{0:T(1024)S(1)} %pad_maximum_fusion.3, s32[13312]{0:T(1024)S(1)} %copy-done.95), kind=kCustom, calls=%fused_computation.10 | custom fusion | bytes 153600 | tf_op jit(solution)/shard_map/jit(_take)/gather | solution.py:226
  1035.7 19.6 %convolution_add_fusion.1 = f32[12800,384]{1,0:T(8,128)} fusion(f32[12800,384]{1,0:T(8,128)} %fusion.277, bf16[384,128]{1,0:T(8,128)(2,1)S(1)} %copy-done.67, f32[12800,128]{1,0:T(8,128)} %copy-done.5), kind=kOutput, calls=%fused_computation.38 | convolution fusion | flops 1269760000 | bytes 45973504 | tf_op jit(solution)/shard_map/dot_general | solution.py:25
  1055.4 37.0 %add_convert_fusion = bf16[32,400,384]{2,1,0:T(8,128)(2,1)} fusion(f32[32,400,384]{2,1,0:T(8,128)} %get-tuple-element.53, f32[32,400,384]{2,1,0:T(8,128)} %bitcast.318, f32[32,400,384]{2,1,0:T(8,128)} %get-tuple-element.72, bf16[32,400,768]{2,1,0:T(8,128)(2,1)} %bitcast.300, bf16[32,384,768]{2,1,0:T(8,128)(2,1)} %param.39), kind=kOutput, calls=%fused_computation.22 | convolution fusion | flops 7623475200 | bytes 107347968 | tf_op jit(solution)/shard_map/ecd,efd->ecf/dot_general | solution.py:234
  1121.4 32.0 %fusion.314 = f32[32,400,768]{2,1,0:T(8,128)} fusion(bf16[32,400,384]{2,1,0:T(8,128)(2,1)} %add_convert_fusion, bf16[32,768,384]{2,1,0:T(8,128)(2,1)} %param.38), kind=kOutput, calls=%fused_computation.466 | convolution fusion | flops 7549747200 | bytes 68026368 | tf_op jit(solution)/shard_map/ecf,edf->ecd/dot_general | solution.py:246
  1153.4 25.1 %gather_fusion.8 = f32[3152,768]{1,0:T(8,128)} fusion(f32[12800,768]{1,0:T(8,128)} %bitcast.298, s32[4096]{0:T(1024)S(1)} %copy-done.92), kind=kCustom, calls=%fused_computation.7.clone | custom fusion | bytes 19378496 | tf_op jit(solution)/shard_map/jit(_take)/gather | solution.py:251
  1178.6 25.1 %gather_fusion.9 = f32[3152,768]{1,0:T(8,128)} fusion(f32[12800,768]{1,0:T(8,128)} %bitcast.299, s32[4096]{0:T(1024)S(1)} %copy-done.90), kind=kCustom, calls=%fused_computation.8.clone | custom fusion | bytes 19378496 | tf_op jit(solution)/shard_map/jit(_take)/gather | solution.py:251
  1262.9 17.0 reduce-scatter.21.cloned.1.call-done
  1327.0 41.9 %fusion.1 = bf16[800,384]{1,0:T(8,128)(2,1)S(1)} fusion(bf16[3152,384]{1,0:T(8,128)(2,1)} %fusion.16), kind=kCustom, calls=%all-reduce-scatter.1 | all-reduce-scatter fusion | flops 1228801 | bytes 3035648
  1450.5 37.7 %all-gather.27.cloned.1.call-done = bf16[4,788,1152]{2,1,0:T(8,128)(2,1)} async-done(((bf16[1,788,1152]{2,1,0:T(8,128)(2,1)}), bf16[4,788,1152]{2,1,0:T(8,128)(2,1)}) %all-gather.27.cloned.1.call-update) | async-done | bytes 7262224 | tf_op jit(solution)/shard_map/all_gather | solution.py:94
  1617.1 119.7 %all-reduce.22.cloned.1.call-done = (f32[768,128]{1,0:T(8,128)}, f32[128,768]{1,0:T(8,128)}) async-done(((f32[768,128]{1,0:T(8,128)}, f32[128,768]{1,0:T(8,128)}), (f32[768,128]{1,0:T(8,128)}, f32[128,768]{1,0:T(8,128)})) %all-reduce.22.cloned.1.call-update) | async-done | bytes 786448 | tf_op jit(solution)/shard_map/psum | solution.py:341
  1736.8 57.5 %all-reduce.26.cloned.1.call-done = (f32[3,192,128]{2,1,0:T(8,128)}, f32[128,192]{0,1:T(8,128)}) async-done(((f32[3,192,128]{2,1,0:T(8,128)}, f32[128,192]{0,1:T(8,128)}), (f32[3,192,128]{2,1,0:T(8,128)}, f32[128,192]{0,1:T(8,128)})) %all-reduce.26.cloned.1.call-update) | async-done | bytes 393232 | tf_op jit(solution)/shard_map/psum | solution.py:334
  1794.3 116.1 %all-reduce.24.cloned.1.call-done = (f32[3,128,384]{2,1,0:T(8,128)}, f32[384,128]{1,0:T(8,128)}) async-done(((f32[3,128,384]{2,1,0:T(8,128)}, f32[384,128]{1,0:T(8,128)}), (f32[3,128,384]{2,1,0:T(8,128)}, f32[384,128]{1,0:T(8,128)})) %all-reduce.24.cloned.1.call-update) | async-done | bytes 786448 | tf_op jit(solution)/shard_map/psum | solution.py:333
  (531 shorter events, 641.9 us)
Async XLA Ops:
  7.2 715.2 %copy-start = (bf16[128,768]{1,0:T(8,128)(2,1)S(1)}, bf16[128,768]{1,0:T(8,128)(2,1)}, u32[]{:S(2)}) copy-start(bf16[128,768]{1,0:T(8,128)(2,1)} %param.49) | copy-start | bytes 589828
  7.2 30.6 %all-gather.21.cloned.1.call-start = ((), (), s32[]{:S(2)}) async-start(), calls=%async_computation.12 | async-start | bytes 1916928 | tf_op jit(solution)/shard_map/all_gather | solution.py:82
  28.9 201.6 %all-gather.23.cloned.1.call-start = ((), (), s32[]{:S(2)}) async-start(), calls=%async_computation.13 | async-start | bytes 3041280 | tf_op jit(solution)/shard_map/all_gather | solution.py:94
  29.2 430.9 %copy-start.51 = (s32[3152]{0:T(1024)}, s32[3152]{0:T(1024)S(1)}, u32[]{:S(2)}) copy-start(s32[3152]{0:T(1024)S(1)} %eq.61) | copy-start | bytes 37828
  29.3 430.9 %copy-start.100 = (s32[128]{0:T(128)}, s32[128]{0:T(128)S(1)}, u32[]{:S(2)}) copy-start(s32[128]{0:T(128)S(1)} %and_select_fusion.2) | copy-start | bytes 1540
  64.8 87.1 %copy-start.119 = (u32[32]{0:T(128)S(1)}, u32[32]{0:T(128)}, u32[]{:S(2)}) copy-start(u32[32]{0:T(128)} %constant.262) | copy-start | bytes 388
  149.4 4.6 collective-permute-start
  190.4 58.2 %reduce-scatter.23.cloned.1.call-start = ((), (), s32[]{:S(2)}) async-start(), calls=%async_computation.16 | async-start | bytes 2420736
  239.4 51.5 %all-gather.17.cloned.1.call-start = ((), (), s32[]{:S(2)}) async-start(), calls=%async_computation.9 | async-start | bytes 3194880 | tf_op jit(solution)/shard_map/all_gather | solution.py:109
  239.9 91.9 %all-gather.13.cloned.1.call-start = ((), (), s32[]{:S(2)}) async-start(), calls=%async_computation.6 | async-start | bytes 3194880 | tf_op jit(solution)/shard_map/all_gather | solution.py:109
  268.2 136.8 %all-gather.19.cloned.1.call-start = ((), (), s32[]{:S(2)}) async-start(), calls=%async_computation.10 | async-start | bytes 7262208 | tf_op jit(solution)/shard_map/all_gather | solution.py:82
  295.4 164.7 %all-gather.15.cloned.1.call-start = ((), (), s32[]{:S(2)}) async-start(), calls=%async_computation.7 | async-start | bytes 7262208 | tf_op jit(solution)/shard_map/all_gather | solution.py:82
  336.4 898.7 %reduce-scatter.27.cloned.1.call-start = ((), (), s32[]{:S(2)}) async-start(), calls=%async_computation.18 | async-start | bytes 7262208
  410.8 49.4 %copy-start.74 = (bf16[768,128]{1,0:T(8,128)(2,1)S(1)}, bf16[768,128]{1,0:T(8,128)(2,1)}, u32[]{:S(2)}) copy-start(bf16[768,128]{1,0:T(8,128)(2,1)} %param.44) | copy-start | bytes 589828
  469.9 49.4 %copy-start.56 = (bf16[768,128]{1,0:T(8,128)(2,1)S(1)}, bf16[768,128]{1,0:T(8,128)(2,1)}, u32[]{:S(2)}) copy-start(bf16[768,128]{1,0:T(8,128)(2,1)} %param.46) | copy-start | bytes 589828
  876.1 48.5 %copy-start.1 = (f32[3152,32]{0,1:T(8,128)}, f32[3152,32]{0,1:T(8,128)S(1)}, u32[]{:S(2)}) copy-start(f32[3152,32]{0,1:T(8,128)S(1)} %get-tuple-element.51) | copy-start | bytes 1210372
  926.8 67.3 %copy-start.93 = (f32[3152,2]{0,1:T(2,128)}, f32[3152,2]{0,1:T(2,128)S(1)}, u32[]{:S(2)}) copy-start(f32[3152,2]{0,1:T(2,128)S(1)} %and_select_fusion.1) | copy-start | bytes 75652
  928.2 66.0 %copy-start.71 = (s32[12800]{0:T(1024)S(1)}, s32[12800]{0:T(1024)}, u32[]{:S(2)}) copy-start(s32[12800]{0:T(1024)} %copy-done.70) | copy-start | bytes 153604
  928.2 66.0 %copy-start.77 = (pred[12800]{0:T(1024)(128)(4,1)S(1)}, pred[12800]{0:T(1024)(128)(4,1)}, u32[]{:S(2)}) copy-start(pred[12800]{0:T(1024)(128)(4,1)} %get-tuple-element.54) | copy-start | bytes 38404
  1221.0 59.0 %reduce-scatter.21.cloned.1.call-start = ((), (), s32[]{:S(2)}) async-start(), calls=%async_computation.11 | async-start | bytes 3194880 | tf_op jit(solution)/shard_map/reduce_scatter | solution.py:115
  1239.6 73.0 %all-gather.25.cloned.1.call-start = ((), (), s32[]{:S(2)}) async-start(), calls=%async_computation.14 | async-start | bytes 1916928 | tf_op jit(solution)/shard_map/all_gather | solution.py:82
  1303.2 185.1 %all-gather.27.cloned.1.call-start = ((), (), s32[]{:S(2)}) async-start(), calls=%async_computation.15 | async-start | bytes 9123840 | tf_op jit(solution)/shard_map/all_gather | solution.py:94
  1368.9 4.0 collective-permute-start.1
  1407.8 102.9 %reduce-scatter.25.cloned.1.call-start = ((), (), s32[]{:S(2)}) async-start(), calls=%async_computation.17 | async-start | bytes 7262208
  1418.0 142.4 %all-reduce.28.cloned.1.call-start = ((), (), s32[]{:S(2)}) async-start(), calls=%async_computation.23 | async-start | bytes 786432 | tf_op jit(solution)/shard_map/psum | solution.py:336
  1450.5 144.1 %reduce-scatter.29.cloned.1.call-start = ((), (), s32[]{:S(2)}) async-start(), calls=%async_computation.19 | async-start | bytes 2420736
  1510.6 102.7 %reduce-scatter.19.cloned.1.call-start = ((), (), s32[]{:S(2)}) async-start(), calls=%async_computation.8 | async-start | bytes 3194880 | tf_op jit(solution)/shard_map/reduce_scatter | solution.py:115
  1515.2 221.5 %all-reduce.22.cloned.1.call-start = ((), (), s32[]{:S(2)}) async-start(), calls=%async_computation.20 | async-start | bytes 1572864 | tf_op jit(solution)/shard_map/psum | solution.py:341
  1560.1 234.2 %all-reduce.26.cloned.1.call-start = ((), (), s32[]{:S(2)}) async-start(), calls=%async_computation.22 | async-start | bytes 786432 | tf_op jit(solution)/shard_map/psum | solution.py:334
  1589.4 321.0 %all-reduce.24.cloned.1.call-start = ((), (), s32[]{:S(2)}) async-start(), calls=%async_computation.21 | async-start | bytes 1572864 | tf_op jit(solution)/shard_map/psum | solution.py:333
  1736.8 180.4 %copy-start.88 = (f32[768,128]{1,0:T(8,128)S(1)}, f32[768,128]{1,0:T(8,128)}, u32[]{:S(2)}) copy-start(f32[768,128]{1,0:T(8,128)} %get-tuple-element.89) | copy-start | bytes 1179652
  1736.8 181.1 %copy-start.87 = (f32[128,768]{1,0:T(8,128)S(1)}, f32[128,768]{1,0:T(8,128)}, u32[]{:S(2)}) copy-start(f32[128,768]{1,0:T(8,128)} %get-tuple-element.92) | copy-start | bytes 1179652
  (123 other events, 1396.9 us)
Sparse Core Ops, SparseCore 0:
  29.0 8.7 all-gather.20
  190.5 39.9 all-gather.22
  239.5 9.1 reduce-scatter.22
  250.5 40.3 all-gather.16
  292.7 39.1 all-gather.12
  333.3 14.5 all-gather.18
  349.6 15.7 all-gather.14
  1221.1 13.9 reduce-scatter.26
  1239.7 40.2 reduce-scatter.20
  1303.3 9.2 all-gather.24
  1407.9 80.3 all-gather.26
  1490.4 13.0 reduce-scatter.24
  1507.4 38.5 all-reduce.27
  1548.1 8.8 reduce-scatter.28
  1560.3 40.2 reduce-scatter.18
  1607.2 129.4 all-reduce.21
  1739.6 54.6 all-reduce.25
  1800.9 109.4 all-reduce.23
where the time goes:
time: 1940 us; the launch traced here: 1930 us
  local copies, waits for them, and re-layouts  568 us (29%)
  matrix products  469 us (24%)
  waiting for transfers between devices  465 us (24%)
  blocking collectives  229 us (12%)
  other arithmetic  170 us (9%)
    dot_general x78, matrix products, matmul(): return jnp.dot(left, right, preferred_element_type=jnp.float32)  329 us
    unnamed x2, blocking collectives  126 us
    psum x1, waiting for transfers between devices, on_device(): all_total = lax.psum((part_a_up, part_b_down), ('dp', 'row', 'col'))  120 us
    psum x1, waiting for transfers between devices, on_device(): col_total = lax.psum((jnp.stack(b_parts), part_a_out), ('dp', 'col'))  116 us
    unnamed x302, local copies, waits for them, and re-layouts  100 us
    all_gather x2, waiting for transfers between devices, col_rows(): return lax.all_gather(values_in, 'col', axis=0, tiled=True)  77.3 us
    gather x1, local copies, waits for them, and re-layouts, on_device(): jnp.take(jnp.concatenate([jnp.zeros((1,), jnp.float32), gate_vals.reshape...  65.9 us
    psum x4, blocking collectives, feature_sums(): return lax.psum((jnp.sum(first, axis=1), jnp.sum(second, axis=1)), 'col')  64 us
  transfers between devices with their start and end apart: 20, of which 14 were waited for; matrix products, arithmetic and copies ran while one was open for 17% of the time, Pallas kernels for 0%

commit v1 on v0

v1 whole, which is shorter than its diff:
```python
import jax
import jax.numpy as jnp
from jax import lax
from jax.experimental import pallas as pl
from jax.experimental.pallas import tpu as pltpu
from jax.sharding import PartitionSpec as P

D = 768
EXPERTS = 32
SEQ = 197
SEQP = 208
RANK = 16
ADAPT = 128
IMG_GRP = 16
TOK = IMG_GRP * SEQP
BLK = 2 * SEQP
DUMMY = SEQ
TILE = 128
f32 = jnp.float32
bf16 = jnp.bfloat16


def dot(left, right):
    return jnp.dot(left, right, preferred_element_type=f32)


def dot_nt(left, right):
    return lax.dot_general(left, right, (((1,), (1,)), ((), ())), preferred_element_type=f32)


def dot_tn(left, right):
    return lax.dot_general(left, right, (((0,), (0,)), ((), ())), preferred_element_type=f32)


def lane_iota(shape):
    return lax.broadcasted_iota(jnp.int32, shape, len(shape) - 1)


def moe_kernel(n_x, n_c, list_ref, offs_ref, picks_ref, *refs):
    x_blocks = refs[:n_x]
    c_blocks = refs[n_x : n_x + n_c]
    (
        w_up, w_down, b_up, a_down, a_up, b_down, w_router, a_router, b_router,
        ep_out, tg_out, gbu_out, gad_out, gau_out, gbd_out,
        xin, cin, gpin, table, acc, rows_in, rows_out, in_sem, ep_sem, tg_sem,
    ) = refs[n_x + n_c :]
    expert = pl.program_id(0)
    half = w_up.shape[2]
    acc_flat = acc.reshape(TOK * 16, 128)
    in_flat = rows_in.reshape(TILE * 16, 128)
    out_flat = rows_out.reshape(TILE * 16, 128)
    lane = lane_iota((1, 128))

    @pl.when(expert == 0)
    def prologue():
        copies = []
        for blocks, place in ((x_blocks, xin), (c_blocks, cin)):
            row = 0
            for block in blocks:
                rows = block.shape[0]
                copies.append(pltpu.make_async_copy(block, place.at[pl.ds(row, rows)], in_sem.at[len(copies)]))
                row += rows
        for copy in copies:
            copy.start()
        rows_in[...] = jnp.zeros_like(rows_in)
        rows_out[...] = jnp.zeros_like(rows_out)
        gbu_out[...] = jnp.zeros_like(gbu_out)
        gad_out[...] = jnp.zeros_like(gad_out)
        gau_out[...] = jnp.zeros_like(gau_out)
        gbd_out[...] = jnp.zeros_like(gbd_out)
        for copy in copies:
            copy.wait()

        def image(i, carry):
            row = pl.multiple_of(i * SEQP, 16)
            mask = (lane // RANK) == picks_ref[i]
            x = xin[pl.ds(row, SEQP), :]
            c = cin[pl.ds(row, SEQP), :]
            low_x = jnp.where(mask, dot(x, a_up[...]), 0.0)
            low_c = jnp.where(mask, dot_nt(c, b_down[...]), 0.0)
            low_r = jnp.where(mask, dot(x, a_router[...]), 0.0).astype(bf16)
            logits = dot(x, w_router[...]) + dot(low_r, b_router[...])
            logits = jnp.where(lane < 2 * EXPERTS, logits, -1e30)
            power = jnp.exp(logits - jnp.max(logits, axis=1, keepdims=True))
            total = jnp.sum(jnp.where(lane < EXPERTS, power, 0.0), axis=1, keepdims=True)
            probs = power / total
            lead = probs.astype(bf16).astype(f32)
            probs = jnp.where(lane < EXPERTS, lead, probs - lead)
            base = row * 16
            for j in range(6):
                acc_flat[pl.ds(base + j, SEQP, 16), :] = x[:, 128 * j : 128 * j + 128].astype(f32)
                acc_flat[pl.ds(base + 8 + j, SEQP, 16), :] = c[:, 128 * j : 128 * j + 128].astype(f32)
            acc_flat[pl.ds(base + 6, SEQP, 16), :] = low_x
            acc_flat[pl.ds(base + 14, SEQP, 16), :] = low_c
            acc_flat[pl.ds(base + 7, SEQP, 16), :] = probs
            acc_flat[pl.ds(base + 15, SEQP, 16), :] = jnp.zeros((SEQP, 128), f32)
            table[pl.ds(row, SEQP)] = acc[pl.ds(row, SEQP)].astype(bf16)
            acc[pl.ds(row, SEQP)] = jnp.zeros((SEQP, 16, 128), f32)
            return carry

        lax.fori_loop(0, IMG_GRP, image, 0)

    first = offs_ref[expert]
    count = offs_ref[expert + 1] - first

    def tile(t, carry):
        base = first + t * TILE
        rest = count - t * TILE
        batches = (jnp.minimum(rest, TILE) + 7) // 8

        def fetch(b, carry):
            for k in range(8):
                i = b * 8 + k
                token = jnp.where(i < rest, list_ref[base + i], DUMMY)
                rows_in[i] = table[token].astype(f32)
            return carry

        lax.fori_loop(0, batches, fetch, 0)

        def columns(start):
            return jnp.concatenate(
                [in_flat[pl.ds(start + j, TILE, 16), :].astype(bf16) for j in range(7)], axis=1
            )

        x = columns(0)
        c = columns(8)
        spread = in_flat[pl.ds(7, TILE, 16), :]
        inside = lax.broadcasted_iota(jnp.int32, (TILE, 1), 0) < rest
        mine = ((lane == expert) | (lane == expert + EXPERTS)) & inside
        gate = jnp.sum(jnp.where(mine, spread, 0.0), axis=1, keepdims=True)
        w_u = w_up[0]
        w_d = w_down[0]
        hidden = dot(x[:, :D], w_u) + dot(x[:, D:], b_up[...])
        cdf = 0.5 + 0.5 * lax.erf(hidden * 0.7071067811865476)
        slope = cdf + hidden * jnp.exp(hidden * hidden * -0.5) * 0.3989422804014327
        act = (hidden * cdf).astype(bf16)
        back = dot_nt(c[:, :D], w_d) + dot_nt(c[:, D:], a_down[...])
        act_f = act.astype(f32)
        gate_grad = jnp.sum(act_f * back, axis=1, keepdims=True)
        grad_hidden = (gate * back * slope).astype(bf16)
        act_gate = (gate * act_f).astype(bf16)
        out_main = dot(act_gate, w_d)
        out_low = dot(act_gate, a_down[...])
        in_main = dot_nt(grad_hidden, w_u)
        in_low = dot_nt(grad_hidden, b_up[...])
        gbu_out[...] += dot_tn(grad_hidden, x[:, D:])
        gad_out[...] += dot_tn(act_gate, c[:, D:])
        for j in range(6):
            out_flat[pl.ds(j, TILE, 16), :] = out_main[:, 128 * j : 128 * j + 128]
            out_flat[pl.ds(8 + j, TILE, 16), :] = in_main[:, 128 * j : 128 * j + 128]
        out_flat[pl.ds(6, TILE, 16), :] = out_low
        out_flat[pl.ds(14, TILE, 16), :] = in_low
        out_flat[pl.ds(15, TILE, 16), :] = jnp.where((lane == expert) & inside, gate_grad, 0.0)

        def give(b, carry):
            tokens = []
            sums = []
            for k in range(8):
                i = b * 8 + k
                token = jnp.where(i < rest, list_ref[base + i], DUMMY)
                tokens.append(token)
                sums.append(acc[token] + rows_out[i])
            for k in range(8):
                acc[tokens[k]] = sums[k]
            return carry

        lax.fori_loop(0, batches, give, 0)
        return carry

    lax.fori_loop(0, (count + TILE - 1) // TILE, tile, 0)

    @pl.when(expert == EXPERTS - 1)
    def epilogue():
        def image(i, carry):
            row = pl.multiple_of(i * SEQP, 16)
            base = row * 16
            mask = (lane // RANK) == picks_ref[i]

            def chunk(j):
                return acc_flat[pl.ds(base + j, SEQP, 16), :]

            x = xin[pl.ds(row, SEQP), :]
            c = cin[pl.ds(row, SEQP), :]
            low_in = jnp.where(mask, chunk(14), 0.0).astype(bf16)
            low_out = jnp.where(mask, chunk(6), 0.0).astype(bf16)
            gau_out[...] += dot_tn(x, low_in)
            gbd_out[...] += dot_tn(c, low_out)
            extra_in = dot_nt(low_in, a_up[...])
            extra_out = dot(low_out, b_down[...])
            for j in range(6):
                at = slice(128 * j, 128 * j + 128)
                cin[pl.ds(row, SEQP), at] = (chunk(8 + j) + extra_in[:, at]).astype(bf16)
                xin[pl.ds(row, SEQP), at] = (chunk(j) + extra_out[:, at]).astype(bf16)
            gpin[pl.ds(row, SEQP), :] = chunk(15).astype(bf16)
            rows = pl.ds(row, SEQP)
            pltpu.make_async_copy(cin.at[rows], tg_out.at[rows, pl.ds(0, D)], tg_sem).start()
            pltpu.make_async_copy(gpin.at[rows], tg_out.at[rows, pl.ds(D, 128)], tg_sem).start()
            pltpu.make_async_copy(xin.at[rows], ep_out.at[rows], ep_sem).start()
            return carry

        lax.fori_loop(0, IMG_GRP, image, 0)
        pltpu.make_async_copy(cin, tg_out.at[:, pl.ds(0, D)], tg_sem).wait()
        pltpu.make_async_copy(gpin, tg_out.at[:, pl.ds(D, 128)], tg_sem).wait()
        pltpu.make_async_copy(xin, ep_out, ep_sem).wait()


def moe_call(token_list, offs, picks, x_blocks, c_blocks, w_up, w_down, b_up, a_down, a_up, b_down, w_router, a_router, b_router):
    half = w_up.shape[2]
    n_x, n_c = len(x_blocks), len(c_blocks)

    def whole(*shape):
        return pl.BlockSpec(shape, lambda e, *_: (0,) * len(shape))

    anywhere = pl.BlockSpec(memory_space=pl.ANY)
    return pl.pallas_call(
        lambda *refs: moe_kernel(n_x, n_c, *refs),
        grid_spec=pltpu.PrefetchScalarGridSpec(
            num_scalar_prefetch=3,
            grid=(EXPERTS,),
            in_specs=[anywhere] * (n_x + n_c)
            + [
                pl.BlockSpec((1, D, half), lambda e, *_: (e, 0, 0)),
                pl.BlockSpec((1, half, D), lambda e, *_: (e, 0, 0)),
                whole(ADAPT, half),
                whole(half, ADAPT),
                whole(D, ADAPT),
                whole(ADAPT, D),
                whole(D, 128),
                whole(D, ADAPT),
                whole(ADAPT, 128),
            ],
            out_specs=[
                anywhere,
                anywhere,
                whole(half, ADAPT),
                whole(half, ADAPT),
                whole(D, ADAPT),
                whole(D, ADAPT),
            ],
            scratch_shapes=[
                pltpu.VMEM((TOK, D), bf16),
                pltpu.VMEM((TOK, D), bf16),
                pltpu.VMEM((TOK, 128), bf16),
                pltpu.VMEM((TOK, 16, 128), bf16),
                pltpu.VMEM((TOK, 16, 128), f32),
                pltpu.VMEM((TILE, 16, 128), f32),
                pltpu.VMEM((TILE, 16, 128), f32),
                pltpu.SemaphoreType.DMA((n_x + n_c,)),
                pltpu.SemaphoreType.DMA,
                pltpu.SemaphoreType.DMA,
            ],
        ),
        out_shape=[
            jax.ShapeDtypeStruct((TOK, D), bf16),
            jax.ShapeDtypeStruct((TOK, D + 128), bf16),
            jax.ShapeDtypeStruct((half, ADAPT), f32),
            jax.ShapeDtypeStruct((half, ADAPT), f32),
            jax.ShapeDtypeStruct((D, ADAPT), f32),
            jax.ShapeDtypeStruct((D, ADAPT), f32),
        ],
        compiler_params=pltpu.CompilerParams(vmem_limit_bytes=62 * 1024 * 1024),
        cost_estimate=pl.CostEstimate(flops=20_000_000_000, bytes_accessed=60_000_000, transcendentals=10_000_000),
    )(token_list, offs, picks, *x_blocks, *c_blocks, w_up, w_down, b_up, a_down, a_up, b_down, w_router, a_router, b_router)


HEADS = 12
HEAD_DIM = 64
PART_ROWS = 7168


def pick_mask(pick):
    return (lane_iota((1, ADAPT)) // RANK) == pick


def norm_stats(values):
    centre = jnp.sum(values, axis=1, keepdims=True) * (1.0 / D)
    shifted = values - centre
    spread = jnp.sum(shifted * shifted, axis=1, keepdims=True) * (1.0 / D)
    inverse = lax.rsqrt(spread + 1e-06)
    return shifted * inverse, inverse


def norm_back(grad, gain, unit, inverse):
    scaled = grad * gain
    total = jnp.sum(scaled, axis=1, keepdims=True) * (1.0 / D)
    along = jnp.sum(scaled * unit, axis=1, keepdims=True) * (1.0 / D)
    return inverse * (scaled - total - unit * along)


def load_weights(place_ref, blocks, scratch, sem):
    qkv, low_a, low_b, out_w, out_a = blocks
    w_qkv, a_qkv, b_qkv, w_out, a_out = scratch
    row, col = place_ref[0], place_ref[1]
    copies = []

    def copy(source, target):
        copies.append(pltpu.make_async_copy(source, target, sem.at[len(copies)]))

    for t in range(2):
        rows_at = pl.multiple_of((row ^ t) * 384, 128)
        for s in range(4):
            at = pl.multiple_of((col ^ s) * 192, 64)
            copy(qkv[4 * t + s], w_qkv.at[:, pl.ds(at, 192), pl.ds(rows_at, 384)])
        copy(low_b[t], b_qkv.at[:, :, pl.ds(rows_at, 384)])
        copy(out_w[t], w_out.at[pl.ds(rows_at, 384), :])
        copy(out_a[t], a_out.at[pl.ds(rows_at, 384), :])
    for s in range(4):
        at = pl.multiple_of((col ^ s) * 192, 64)
        copy(low_a[s], a_qkv.at[:, pl.ds(at, 192), :])
    for one in copies:
        one.start()
    for one in copies:
        one.wait()


N_COPIES = 18
WEIGHT_SCRATCH = [
    pltpu.VMEM((3, D, D), bf16),
    pltpu.VMEM((3, D, ADAPT), bf16),
    pltpu.VMEM((3, ADAPT, D), bf16),
    pltpu.VMEM((D, D), bf16),
    pltpu.VMEM((D, ADAPT), bf16),
    pltpu.SemaphoreType.DMA((N_COPIES,)),
]


def split_blocks(refs):
    qkv, refs = refs[:8], refs[8:]
    low_a, refs = refs[:4], refs[4:]
    low_b, refs = refs[:2], refs[2:]
    out_w, refs = refs[:2], refs[2:]
    out_a, refs = refs[:2], refs[2:]
    return (qkv, low_a, low_b, out_w, out_a), refs


def attend_kernel(picks_ref, place_ref, *refs):
    blocks, refs = split_blocks(refs)
    (
        x_ref, gain_one, gain_two, b_out,
        two_out, resid_out, normed_out, qkv_out, mixed_out, probs_out, lows_out,
        w_qkv, a_qkv, b_qkv, w_out, a_out, sem,
    ) = refs
    image = pl.program_id(0)

    @pl.when(image == 0)
    def start():
        load_weights(place_ref, blocks, (w_qkv, a_qkv, b_qkv, w_out, a_out), sem)

    mask = pick_mask(picks_ref[image])
    x = x_ref[...].astype(f32)
    unit, unused = norm_stats(x)
    normed = (unit * gain_one[...]).astype(bf16)
    normed_out[...] = normed
    for p in range(3):
        low = jnp.where(mask, dot(normed, a_qkv[p]), 0.0).astype(bf16)
        lows_out[:, 128 * p : 128 * p + 128] = low
        qkv_out[p] = (dot(normed, w_qkv[p]) + dot(low, b_qkv[p])).astype(bf16)
    lane = lane_iota((1, 128))
    key_lane = lane_iota((1, SEQP))
    for pair in range(HEADS // 2):
        at = slice(128 * pair, 128 * pair + 128)
        q = qkv_out[0, :, at]
        k = qkv_out[1, :, at]
        v = qkv_out[2, :, at]
        parts = []
        for side in range(2):
            own = (lane // HEAD_DIM) == side
            scores = dot_nt(jnp.where(own, q, jnp.zeros_like(q)), k) * (HEAD_DIM**-0.5)
            scores = jnp.where(key_lane < SEQ, scores, -1e30)
            power = jnp.exp(scores - jnp.max(scores, axis=1, keepdims=True))
            probs = (power / jnp.sum(power, axis=1, keepdims=True)).astype(bf16)
            probs_out[0, 2 * pair + side] = probs
            parts.append(dot(probs, v))
        mixed_out[:, at] = jnp.where(lane < HEAD_DIM, parts[0], parts[1]).astype(bf16)
    mixed = mixed_out[...]
    low = jnp.where(mask, dot(mixed, a_out[...]), 0.0).astype(bf16)
    lows_out[:, 384:512] = low
    resid = x + dot(mixed, w_out[...]) + dot(low, b_out[...])
    resid_out[...] = resid
    unit, unused = norm_stats(resid)
    two_out[...] = (unit * gain_two[...]).astype(bf16)


def image_rows(lanes):
    return pl.BlockSpec((SEQP, lanes), lambda i, *_: (i, 0))


def kept(*shape):
    return pl.BlockSpec(shape, lambda i, *_: (0,) * len(shape))


QKV_SPEC = pl.BlockSpec((3, SEQP, D), lambda i, *_: (0, i, 0))
PROBS_SPEC = pl.BlockSpec((1, HEADS, SEQP, SEQP), lambda i, *_: (i, 0, 0, 0))
ANYWHERE = pl.BlockSpec(memory_space=pl.ANY)


def attend_call(picks, place, blocks, x, gain_one, gain_two, b_out):
    rows = x.shape[0]
    return pl.pallas_call(
        attend_kernel,
        grid_spec=pltpu.PrefetchScalarGridSpec(
            num_scalar_prefetch=2,
            grid=(2,),
            in_specs=[ANYWHERE] * len(blocks)
            + [image_rows(D), kept(1, D), kept(1, D), kept(ADAPT, D)],
            out_specs=[
                image_rows(D), image_rows(D), image_rows(D), QKV_SPEC,
                image_rows(D), PROBS_SPEC, image_rows(512),
            ],
            scratch_shapes=WEIGHT_SCRATCH,
        ),
        out_shape=[
            jax.ShapeDtypeStruct((rows, D), bf16),
            jax.ShapeDtypeStruct((rows, D), f32),
            jax.ShapeDtypeStruct((rows, D), bf16),
            jax.ShapeDtypeStruct((3, rows, D), bf16),
            jax.ShapeDtypeStruct((rows, D), bf16),
            jax.ShapeDtypeStruct((2, HEADS, SEQP, SEQP), bf16),
            jax.ShapeDtypeStruct((rows, 512), bf16),
        ],
        compiler_params=pltpu.CompilerParams(vmem_limit_bytes=48 * 1024 * 1024),
        cost_estimate=pl.CostEstimate(flops=4_000_000_000, bytes_accessed=15_000_000, transcendentals=2_000_000),
    )(picks, place, *blocks, x, gain_one, gain_two, b_out)


def attend_back_kernel(picks_ref, place_ref, *refs):
    blocks, refs = split_blocks(refs)
    (
        x_ref, gain_one, gain_two, b_out,
        two_ref, resid_ref, normed_ref, qkv_ref, mixed_ref, probs_ref, lows_ref,
        cot_ref, grad_a, grad_b, w_router, a_router, b_router,
        tokens_out, parts_out,
        w_qkv, a_qkv, b_qkv, w_out, a_out, sem, parts, grads, grad_mixed,
    ) = refs
    image = pl.program_id(0)

    @pl.when(image == 0)
    def start():
        parts[...] = jnp.zeros_like(parts)
        load_weights(place_ref, blocks, (w_qkv, a_qkv, b_qkv, w_out, a_out), sem)

    mask = pick_mask(picks_ref[image])
    lane = lane_iota((1, 128))

    def add_part(row, value):
        at = slice(row, row + value.shape[0])
        parts[at, :] += value

    two = two_ref[...]
    received = grad_a[...].astype(f32) + grad_b[...].astype(f32)
    low_r = jnp.where(mask, dot(two, a_router[...]), 0.0).astype(bf16)
    logits = dot(two, w_router[...]) + dot(low_r, b_router[...])
    logits = jnp.where(lane < EXPERTS, logits, -1e30)
    power = jnp.exp(logits - jnp.max(logits, axis=1, keepdims=True))
    probs = power / jnp.sum(power, axis=1, keepdims=True)
    grad_probs = jnp.where(lane < EXPERTS, received[:, D:], 0.0)
    grad_logits = probs * (grad_probs - jnp.sum(probs * grad_probs, axis=1, keepdims=True))
    grad_logits = grad_logits.astype(bf16)
    grad_low = jnp.where(mask, dot_nt(grad_logits, b_router[...]), 0.0).astype(bf16)
    grad_two = received[:, :D] + dot_nt(grad_logits, w_router[...]) + dot_nt(grad_low, a_router[...])
    add_part(6144, dot_tn(two, grad_low))
    add_part(6912, dot_tn(grad_logits, low_r))
    unit, inverse = norm_stats(resid_ref[...])
    grad_resid = cot_ref[...].astype(f32) + norm_back(grad_two, gain_two[...], unit, inverse)
    grad_attn = grad_resid.astype(bf16)
    mixed = mixed_ref[...]
    grad_low = jnp.where(mask, dot_nt(grad_attn, b_out[...]), 0.0).astype(bf16)
    grad_mixed[...] = (dot_nt(grad_attn, w_out[...]) + dot_nt(grad_low, a_out[...])).astype(bf16)
    add_part(4608, dot_tn(mixed, grad_low))
    add_part(5376, dot_tn(grad_attn, lows_ref[:, 384:512]))
    for pair in range(HEADS // 2):
        at = slice(128 * pair, 128 * pair + 128)
        q = qkv_ref[0, :, at]
        k = qkv_ref[1, :, at]
        v = qkv_ref[2, :, at]
        gm = grad_mixed[:, at]
        found = []
        for side in range(2):
            own = (lane // HEAD_DIM) == side
            weights = probs_ref[0, 2 * pair + side]
            weights_f = weights.astype(f32)
            grad_w = dot_nt(jnp.where(own, gm, jnp.zeros_like(gm)), v)
            inner = jnp.sum(weights_f * grad_w, axis=1, keepdims=True)
            grad_s = (weights_f * (grad_w - inner)).astype(bf16)
            found.append(
                (
                    dot(grad_s, k) * (HEAD_DIM**-0.5),
                    dot_tn(grad_s, q) * (HEAD_DIM**-0.5),
                    dot_tn(weights, gm),
                )
            )
        for p in range(3):
            grads[p, :, at] = jnp.where(lane < HEAD_DIM, found[0][p], found[1][p]).astype(bf16)
    normed = normed_ref[...]
    grad_normed = jnp.zeros((SEQP, D), f32)
    for p in range(3):
        piece = grads[p]
        grad_low = jnp.where(mask, dot_nt(piece, b_qkv[p]), 0.0).astype(bf16)
        grad_normed = grad_normed + dot_nt(piece, w_qkv[p]) + dot_nt(grad_low, a_qkv[p])
        add_part(768 * p, dot_tn(normed, grad_low))
        add_part(2304 + 768 * p, dot_tn(piece, lows_ref[:, 128 * p : 128 * p + 128]))
    unit, inverse = norm_stats(x_ref[...].astype(f32))
    tokens_out[...] = (grad_resid + norm_back(grad_normed, gain_one[...], unit, inverse)).astype(bf16)

    @pl.when(image == 1)
    def finish():
        parts_out[...] = parts[...].astype(bf16)


def attend_back_call(picks, place, blocks, x, gain_one, gain_two, b_out, saved, cot, grad_a, grad_b, w_router, a_router, b_router):
    rows = x.shape[0]
    return pl.pallas_call(
        attend_back_kernel,
        grid_spec=pltpu.PrefetchScalarGridSpec(
            num_scalar_prefetch=2,
            grid=(2,),
            in_specs=[ANYWHERE] * len(blocks)
            + [image_rows(D), kept(1, D), kept(1, D), kept(ADAPT, D)]
            + [
                image_rows(D), image_rows(D), image_rows(D), QKV_SPEC,
                image_rows(D), PROBS_SPEC, image_rows(512),
            ]
            + [image_rows(D), image_rows(D + 128), image_rows(D + 128)]
            + [kept(D, 128), kept(D, ADAPT), kept(ADAPT, 128)],
            out_specs=[image_rows(D), kept(PART_ROWS, 128)],
            scratch_shapes=WEIGHT_SCRATCH
            + [
                pltpu.VMEM((PART_ROWS, 128), f32),
                pltpu.VMEM((3, SEQP, D), bf16),
                pltpu.VMEM((SEQP, D), bf16),
            ],
        ),
        out_shape=[
            jax.ShapeDtypeStruct((rows, D), bf16),
            jax.ShapeDtypeStruct((PART_ROWS, 128), bf16),
        ],
        compiler_params=pltpu.CompilerParams(vmem_limit_bytes=56 * 1024 * 1024),
        cost_estimate=pl.CostEstimate(flops=9_000_000_000, bytes_accessed=20_000_000, transcendentals=100_000),
    )(picks, place, *blocks, x, gain_one, gain_two, b_out, *saved, cot, grad_a, grad_b, w_router, a_router, b_router)


def across_row(value):
    return lax.ppermute(value, "row", [(0, 1), (1, 0)])


def across_col(value, step):
    return lax.ppermute(value, "col", [(i, i ^ step) for i in range(4)])


def by_place(blocks, col):
    found = []
    for place in range(4):
        value = blocks[place]
        for other in range(1, 4):
            value = jnp.where(col == other, blocks[place ^ other], value)
        found.append(value)
    return found


def gather_col(value, axis=0):
    middle = value.shape[axis] // 2
    from_x = across_col(value, 1)
    from_y = across_col(value, 2)
    head = across_col(lax.slice_in_dim(from_y, 0, middle, axis=axis), 1)
    tail = across_col(lax.slice_in_dim(from_x, middle, 2 * middle, axis=axis), 2)
    return [value, from_x, from_y, head, tail]


def joined(blocks, axis=0):
    return blocks[:3] + [jnp.concatenate(blocks[3:], axis=axis)]


def gather_group(value):
    own = gather_col(value)
    return own + [across_row(block) for block in own]


def added(*values):
    total = values[0].astype(f32)
    for value in values[1:]:
        total = total + value.astype(f32)
    return total


def scatter_group(value):
    lanes = value.shape[1]
    both = added(value[: TOK // 2], across_row(value[TOK // 2 :])).astype(bf16)
    both = both.reshape(4, 2, SEQP, lanes)
    from_x = across_col(jnp.stack([both[1, 0], both[3, 0]]), 1)
    from_y = across_col(jnp.stack([both[2, 1], both[3, 1]]), 2)
    last_y = across_col(added(both[2, 0], from_x[1]).astype(bf16), 2)
    last_x = across_col(added(both[1, 1], from_y[1]).astype(bf16), 1)
    mine = jnp.concatenate([added(both[0, 0], from_x[0]), added(both[0, 1], from_y[0])])
    return mine.astype(bf16), jnp.concatenate([last_y, last_x])


def reduce_parts(value, row, col):
    n = value.shape[0] // 8
    view = value.reshape(2, 4, n, 128)
    theirs = lax.dynamic_index_in_dim(view, 1 - row, 0, keepdims=False)
    ours = lax.dynamic_index_in_dim(view, row, 0, keepdims=False)
    both = added(ours, across_row(theirs)).astype(bf16)
    found = [lax.dynamic_index_in_dim(both, col, 0, keepdims=False)]
    for s in range(1, 4):
        found.append(across_col(lax.dynamic_index_in_dim(both, col ^ s, 0, keepdims=False), s))
    return added(*found).astype(bf16)


def reduce_dp(value):
    n_dp = lax.axis_size("dp")
    if n_dp != 4:
        return lax.psum(value, "dp")
    place = lax.axis_index("dp")

    def across(part, step):
        return lax.ppermute(part, "dp", [(i, i ^ step) for i in range(4)])

    view = value.reshape(4, -1, 128)
    found = [lax.dynamic_index_in_dim(view, place, 0, keepdims=False)]
    for s in range(1, 4):
        found.append(across(lax.dynamic_index_in_dim(view, place ^ s, 0, keepdims=False), s))
    total = added(*found).astype(bf16)
    blocks = [total] + [across(total, s) for s in range(1, 4)]
    return jnp.concatenate(by_place(blocks, place))


def spread_parts(value, row, col):
    blocks = [value] + [across_col(value, s) for s in range(1, 4)]
    half = jnp.concatenate(by_place(blocks, col))
    other = across_row(half)
    return jnp.where(row == 0, jnp.concatenate([half, other]), jnp.concatenate([other, half]))


def token_blocks(value):
    images = value.reshape(8, SEQ, value.shape[1])
    return jnp.pad(images, ((0, 0), (0, SEQP - SEQ), (0, 0))).reshape(4, BLK, value.shape[1])


def to_features(value, col):
    width = D // 4
    chunks = by_place([value[:, width * p : width * p + width] for p in range(4)], col)
    sent = [jnp.concatenate([chunk[:SEQP], chunk[SEQP:]], axis=1) for chunk in chunks]
    got = [sent[0]] + [across_col(sent[s], s) for s in range(1, 4)]
    rows = []
    for block in by_place(got, col):
        rows += [block[:SEQ, :width], block[:SEQ, width:]]
    return jnp.concatenate(rows, axis=0)


def on_device(
    tokens, cotangent, routes, adapter_pick, gain_attn, gain_moe, w_qkv, w_out, w_router, w_up, w_down,
    a_qkv, b_qkv, a_out, b_out, a_router, b_router, a_up, b_up, a_down, b_down,
):
    row = lax.axis_index("row")
    col = lax.axis_index("col")
    me = row * 4 + col
    place = jnp.stack([row, col]).astype(jnp.int32)

    both = jnp.concatenate([token_blocks(tokens), token_blocks(cotangent)], axis=2)
    pairs = [lax.dynamic_index_in_dim(both, col, 0, keepdims=False)]
    for s in range(1, 4):
        pairs.append(across_col(lax.dynamic_index_in_dim(both, col ^ s, 0, keepdims=False), s))
    pairs = by_place(pairs, col)
    width = D // 4
    x = jnp.concatenate([pair[:, :width] for pair in pairs], axis=1)
    cot = jnp.concatenate([pair[:, width:] for pair in pairs], axis=1)

    own_qkv = joined(gather_col(w_qkv, axis=1), axis=1)
    qkv_blocks = own_qkv + [across_row(block) for block in own_qkv]
    low_a = joined(gather_col(a_qkv, axis=1), axis=1)
    low_b = [b_qkv, across_row(b_qkv)]
    gains = []
    for gain in (gain_attn, gain_moe):
        left = gain
        for unused in range(3):
            lead = lax.reduce_precision(left, 8, 7)
            gains.append(lead.astype(bf16))
            left = left - lead
    small = jnp.concatenate([w_out, b_out, jnp.stack(gains), jnp.zeros((10, width), bf16)], axis=0)
    small = jnp.concatenate([small[:264], small[264:]], axis=1)
    small = by_place([small] + [across_col(small, s) for s in range(1, 4)], col)
    small = jnp.concatenate(
        [jnp.concatenate([block[:, :width] for block in small], axis=1),
         jnp.concatenate([block[:, width:] for block in small], axis=1)], axis=0
    )
    out_w = [small[:384], across_row(small[:384])]
    full_b_out = small[384:512]
    gain_rows = small[512:518].astype(f32)
    gain_one = jnp.sum(gain_rows[:3], axis=0, keepdims=True)
    gain_two = jnp.sum(gain_rows[3:], axis=0, keepdims=True)
    out_a = [a_out, across_row(a_out)]
    blocks = qkv_blocks + low_a + low_b + out_w + out_a

    picks_group = lax.dynamic_slice_in_dim(adapter_pick, lax.axis_index("dp") * IMG_GRP, IMG_GRP)
    order = jnp.arange(IMG_GRP, dtype=jnp.int32)
    picks = jnp.take(picks_group, ((order // 2) ^ me) * 2 + order % 2)
    token = jnp.arange(IMG_GRP * SEQ, dtype=jnp.int32)
    image = token // SEQ
    spot = ((image // 2) ^ me) * BLK + (image % 2) * SEQP + token % SEQ
    keys = (routes * 4096 + spot[:, None]).reshape(-1)
    token_list = jnp.concatenate([lax.sort(keys) & 4095, jnp.zeros((TILE,), jnp.int32)])
    offs = jnp.sum(
        (routes.reshape(-1)[:, None] < jnp.arange(EXPERTS + 1, dtype=jnp.int32)[None, :]).astype(jnp.int32), axis=0
    )
    wide_router = jnp.concatenate([w_router, w_router, jnp.zeros((D, 64), bf16)], axis=1)
    wide_b_router = jnp.concatenate([b_router, b_router, jnp.zeros((ADAPT, 64), bf16)], axis=1)
    slim_router = jnp.concatenate([w_router, jnp.zeros((D, 96), bf16)], axis=1)
    slim_b_router = jnp.concatenate([b_router, jnp.zeros((ADAPT, 96), bf16)], axis=1)

    saved = attend_call(picks, place, blocks, x, gain_one, gain_two, full_b_out)
    cot_blocks = gather_group(cot)
    two_blocks = gather_group(saved[0])
    sums, grads, part_b_up, part_a_down, part_a_up, part_b_down = moe_call(
        token_list, offs, picks, two_blocks, cot_blocks, w_up, w_down, b_up, a_down, a_up, b_down,
        wide_router, a_router, wide_b_router,
    )
    grad_a, grad_b = scatter_group(grads)
    grad_tokens, parts = attend_back_call(
        picks, place, blocks, x, gain_one, gain_two, full_b_out, saved, cot, grad_a, grad_b,
        slim_router, a_router, slim_b_router,
    )
    sum_a, sum_b = scatter_group(sums)
    block_out = to_features((saved[1] + added(sum_a, sum_b)).astype(bf16), col)
    grad_tokens = to_features(grad_tokens, col).astype(f32)

    early = reduce_parts(jnp.concatenate([part_a_up, part_b_down]).astype(bf16), row, col)
    n_early = early.shape[0]
    early = reduce_dp(jnp.concatenate([early, part_b_up.astype(bf16), part_a_down.astype(bf16)]))
    grad_b_up = early[n_early : n_early + 384].astype(f32).T
    grad_a_down = early[n_early + 384 :].astype(f32)
    early = spread_parts(early[:n_early], row, col).astype(f32)

    late = spread_parts(reduce_dp(reduce_parts(parts, row, col)), row, col)
    half = D // 2
    grad_a_qkv = lax.dynamic_slice_in_dim(late[:2304].reshape(3, D, ADAPT), col * width, width, axis=1)
    grad_b_qkv = lax.dynamic_slice_in_dim(late[2304:4608].reshape(3, D, ADAPT), row * half, half, axis=1)
    grad_a_out = lax.dynamic_slice_in_dim(late[4608:5376], row * half, half, axis=0)
    grad_b_out = lax.dynamic_slice_in_dim(late[5376:6144], col * width, width, axis=0)
    return (
        block_out,
        grad_tokens,
        grad_a_qkv.astype(f32),
        jnp.swapaxes(grad_b_qkv.astype(f32), 1, 2),
        grad_a_out.astype(f32),
        grad_b_out.astype(f32).T,
        late[6144:6912].astype(f32),
        late[6912:6944].astype(f32).T,
        early[:768],
        grad_b_up,
        grad_a_down,
        early[768:].T,
    )


def solution(mesh):
    return jax.shard_map(
        on_device,
        mesh=mesh,
        in_specs=(
            P(("dp", "row"), "col"),
            P(("dp", "row"), "col"),
            P("dp", None),
            P(),
            P("col"),
            P("col"),
            P(None, "col", "row"),
            P("row", "col"),
            P(),
            P(None, None, ("row", "col")),
            P(None, ("row", "col"), None),
            P(None, "col", None),
            P(None, None, "row"),
            P("row", None),
            P(None, "col"),
            P(),
            P(),
            P(),
            P(None, ("row", "col")),
            P(("row", "col"), None),
            P(),
        ),
        out_specs=(
            P(("dp", "row"), "col"),
            P(("dp", "row"), "col"),
            P(None, "col", None),
            P(None, None, "row"),
            P("row", None),
            P(None, "col"),
            P(),
            P(),
            P(),
            P(None, ("row", "col")),
            P(("row", "col"), None),
            P(),
        ),
        check_vma=False,
    )
```

time: 1940 us -> 509 us (0.26)
  local copies, waits for them, and re-layouts: 568 us -> 46.5 us
  matrix products: 469 us -> 0 us
  waiting for transfers between devices: 465 us -> 140 us
  blocking collectives: 229 us -> 0 us
  Pallas kernels: 0 us -> 196 us
  other arithmetic: 170 us -> 37.4 us
  starting transfers between devices: 7.2 us -> 80.3 us
    dot_general x89 -> x0, matrix products: 469 us -> none  [the longest x78 329 us: matmul(): return jnp.dot(left, right, preferred_element_type=jnp.float32)]
    gather x16 -> x1, local copies, waits for them, and re-layouts: 386 us -> 0.66 us  [on_device(): picks = jnp.take(picks_group, (order // 2 ^ me) * 2 + order % 2)]
    psum x4 -> x0, waiting for transfers between devices: 293 us -> none  [the longest x1 120 us: on_device(): all_total = lax.psum((part_a_up, part_b_down), ('dp', 'row', 'col'))]
    pallas_call x0 -> x3, Pallas kernels: none -> 196 us  [the longest x1 154 us: moe_call(): pl.pallas_call(lambda *refs: moe_kernel(n_x, n_c, *refs), grid_spec=pltpu...]
    ppermute x0 -> x83, waiting for transfers between devices: none -> 140 us  [the longest x48 129 us: across_col(): return lax.ppermute(value, 'col', [(i, i ^ step) for i in range(4)])]
    all_gather x8 -> x0, waiting for transfers between devices: 129 us -> none  [the longest x2 77.3 us: col_rows(): return lax.all_gather(values_in, 'col', axis=0, tiled=True)]
    unnamed x2 -> x0, blocking collectives: 126 us -> none
    psum x6 -> x0, blocking collectives: 102 us -> none  [the longest x4 64 us: feature_sums(): return lax.psum((jnp.sum(first, axis=1), jnp.sum(second, axis=1)), 'col')]
  transfers between devices with their start and end apart: 20 -> 83, of which waited for: 14 -> 39; matrix products, arithmetic and copies ran while one was open for 17% -> 12% of each run, Pallas kernels for 0% -> 3%
where the time goes in v1:
time: 509 us; the launch traced here: 502 us
  Pallas kernels  196 us (39%)
  waiting for transfers between devices  140 us (28%)
  starting transfers between devices  80.3 us (16%)
  local copies, waits for them, and re-layouts  46.5 us (9%)
  other arithmetic  37.4 us (7%)
    pallas_call x1, Pallas kernels, moe_call(): pl.pallas_call(lambda *refs: moe_kernel(n_x, n_c, *refs), grid_spec=pltpu...  154 us
    ppermute x48, waiting for transfers between devices, across_col(): return lax.ppermute(value, 'col', [(i, i ^ step) for i in range(4)])  129 us
    ppermute x48, starting transfers between devices, across_col(): return lax.ppermute(value, 'col', [(i, i ^ step) for i in range(4)])  56.6 us
    pallas_call x1, Pallas kernels, attend_back_call(): pl.pallas_call(attend_back_kernel, grid_spec=pltpu.PrefetchScalarGridSpec...  27.4 us
    ppermute x12, starting transfers between devices, across(): return lax.ppermute(part, 'dp', [(i, i ^ step) for i in range(4)])  19.7 us
    pallas_call x1, Pallas kernels, attend_call(): pl.pallas_call(attend_kernel, grid_spec=pltpu.PrefetchScalarGridSpec(num_...  14 us
    unnamed x121, local copies, waits for them, and re-layouts  13.3 us
    ppermute x12, waiting for transfers between devices, across(): return lax.ppermute(part, 'dp', [(i, i ^ step) for i in range(4)])  10.9 us
  transfers between devices with their start and end apart: 83, of which 39 were waited for; matrix products, arithmetic and copies ran while one was open for 12% of the time, Pallas kernels for 3%

profile of v1, /device:TPU:0, one launch (start us, length us, event | category | flops | bytes accessed | tf_op | source)
XLA Modules:
  0.0 502.1 jit_solution(11802453758628335750)
XLA Ops:
  5.2 3.9 collective-permute-start.13
  19.0 2.9 collective-permute-done.9.refs_10_
  30.2 10.7 %collective-permute-done.10 = bf16[3,96,128]{2,1,0:T(8,128)(2,1)S(1)} collective-permute-done((bf16[3,96,128]{2,1,0:T(8,128)(2,1)S(1)}, bf16[3,96,128]{2,1,0:T(8,128)(2,1)S(1)}, u32[]{:S(2)}, u32[]{:S(2)}) %collective-permute-start.10) | collective-permute-done | bytes 73760 | tf_op jit(solution)/shard_map/ppermute | solution.py:547
  41.3 8.9 %collective-permute-done.11 = bf16[3,96,128]{2,1,0:T(8,128)(2,1)S(1)} collective-permute-done((bf16[3,96,128]{2,1,0:T(8,128)(2,1)S(1)}, bf16[3,96,128]{2,1,0:T(8,128)(2,1)S(1)}, u32[]{:S(2)}, u32[]{:S(2)}) %collective-permute-start.11) | collective-permute-done | bytes 73760 | tf_op jit(solution)/shard_map/ppermute | solution.py:547
  53.4 9.7 %collective-permute-done.refs_1_ = bf16[3,192,384]{2,1,0:T(8,128)(2,1)S(1)} collective-permute-done((bf16[3,192,384]{2,1,0:T(8,128)(2,1)S(1)}, bf16[3,192,384]{2,1,0:T(8,128)(2,1)S(1)}, u32[]{:S(2)}, u32[]{:S(2)}) %collective-permute-start) | collective-permute-done | bytes 442400 | tf_op jit(solution)/shard_map/ppermute | solution.py:547
  67.0 2.2 collective-permute-done.3
  74.1 14.0 %shard_map.292 = (bf16[416,768]{1,0:T(8,128)(2,1)}, f32[416,768]{1,0:T(8,128)}, bf16[416,768]{1,0:T(8,128)(2,1)}, bf16[3,416,768]{2,1,0:T(8,128)(2,1)}, bf16[416...) custom-call(s32[16]{0:T(128)S(1)} %and_select_fusion.2.picks_ref.refs_2_, ...), custom_call_target="tpu_custom_call" | custom-call | flops 4000000000 | bytes 15000000 | tf_op jit(solution)/shard_map/pallas_call | solution.py:399
  95.3 18.2 %collective-permute-done.32.refs_16_ = bf16[208,768]{1,0:T(8,128)(2,1)} collective-permute-done((bf16[208,768]{1,0:T(8,128)(2,1)S(1)}, bf16[208,768]{1,0:T(8,128)(2,1)}, u32[]{:S(2)}, u32[]{:S(2)}) %collective-permute-start.32) | collective-permute-done | bytes 319520 | tf_op jit(solution)/shard_map/ppermute | solution.py:547
  116.3 7.1 %sort.14 = (s32[6304]{0:T(1024)S(1)}, s32[6304]{0:T(1024)}) sort(s32[6304]{0:T(1024)S(1)} %reshape.232, s32[6304]{0:T(1024)S(1)} %iota.29), dimensions={0}, to_apply=%region_2.3 | sort | flops 81952 | bytes 100864 | tf_op jit(solution)/shard_map/sort | solution.py:701
  131.4 4.1 collective-permute-done.23.refs_6_
  138.8 154.3 %shard_map.293 = (bf16[3328,768]{1,0:T(8,128)(2,1)}, bf16[3328,896]{1,0:T(8,128)(2,1)}, f32[384,128]{1,0:T(8,128)}, f32[384,128]{1,0:T(8,128)}, f32[768,128]{1,0:T(8,128)}, /*index=5*/f32[768,128]{1,0:T(8,128)}) custom-call(s32[6432]{0:T(1024)} %concatenate.137.refs_0_, s32[33]{0:T(128)} %convert_reduce_fusion.refs_1_, s32[16]{0:T(128)} %copy-done.22, ...), custom_call_target="tpu_custom_call" | custom-call | flops 20000000000 | bytes 60000000 | tf_op jit(solution)/shard_map/pallas_call | solution.py:215
  295.8 3.5 slice.365
  306.8 3.8 collective-permute-start.73
  313.3 3.7 slice.399
  322.0 2.4 collective-permute-done.76
  324.4 2.3 collective-permute-done.77
  337.7 3.3 add_convert_fusion.1
  343.4 2.7 add_convert_fusion
  346.0 12.0 %collective-permute-done.41 = bf16[2,208,768]{2,1,0:T(8,128)(2,1)S(1)} collective-permute-done((bf16[2,208,768]{2,1,0:T(8,128)(2,1)S(1)}, bf16[2,208,768]{2,1,0:T(8,128)(2,1)S(1)}, u32[]{:S(2)}, u32[]{:S(2)}) %collective-permute-start.41) | collective-permute-done | bytes 639008 | tf_op jit(solution)/shard_map/ppermute | solution.py:547
  363.6 6.0 %collective-permute-done.42 = bf16[208,768]{1,0:T(8,128)(2,1)S(1)} collective-permute-done((bf16[208,768]{1,0:T(8,128)(2,1)S(1)}, bf16[208,768]{1,0:T(8,128)(2,1)S(1)}, u32[]{:S(2)}, u32[]{:S(2)}) %collective-permute-start.42) | collective-permute-done | bytes 319520 | tf_op jit(solution)/shard_map/ppermute | solution.py:547
  375.3 15.0 %collective-permute-done.44 = bf16[208,384]{1,0:T(8,128)(2,1)S(1)} collective-permute-done((bf16[208,384]{1,0:T(8,128)(2,1)S(1)}, bf16[208,384]{1,0:T(8,128)(2,1)S(1)}, u32[]{:S(2)}, u32[]{:S(2)}) %collective-permute-start.44) | collective-permute-done | bytes 159776 | tf_op jit(solution)/shard_map/ppermute | solution.py:547
  394.8 2.3 concatenate.147
  399.2 2.2 collective-permute-done.50
  404.0 27.4 %shard_map.294 = (bf16[416,768]{1,0:T(8,128)(2,1)}, bf16[7168,128]{1,0:T(8,128)(2,1)}) custom-call(s32[16]{0:T(128)} %copy-done.22, s32[2]{0:T(128)} %copy-done.23, bf16[3,192,384]{2,1,0:T(8,128)(2,1)} %refs_0_.3, bf16[3,192,384]{2,1,0:T(8,128)(2,1)} %copy-done.5, bf16[3,192,384]{2,1,0:T(8,128)(2,1)} %copy-done.4, bf16[3,192,384]{2,1,0:T(8,128)(2,1)} %copy-done.6, ...), custom_call_target="tpu_custom_call" | custom-call | flops 8999999488 | bytes 20000000 | tf_op jit(solution)/shard_map/pallas_call | solution.py:512
  440.0 5.8 %collective-permute-done.56 = bf16[896,128]{1,0:T(8,128)(2,1)S(1)} collective-permute-done((bf16[896,128]{1,0:T(8,128)(2,1)S(1)}, bf16[896,128]{1,0:T(8,128)(2,1)S(1)}, u32[]{:S(2)}, u32[]{:S(2)}) %collective-permute-start.56) | collective-permute-done | bytes 229408 | tf_op jit(solution)/shard_map/ppermute | solution.py:547
  445.7 8.2 %collective-permute-done.57 = bf16[896,128]{1,0:T(8,128)(2,1)S(1)} collective-permute-done((bf16[896,128]{1,0:T(8,128)(2,1)S(1)}, bf16[896,128]{1,0:T(8,128)(2,1)S(1)}, u32[]{:S(2)}, u32[]{:S(2)}) %collective-permute-start.57) | collective-permute-done | bytes 229408 | tf_op jit(solution)/shard_map/ppermute | solution.py:547
  454.2 2.1 collective-permute-start.60
  456.2 2.3 collective-permute-start.61
  459.1 2.4 collective-permute-done.60
  462.3 2.4 collective-permute-start.62
  475.5 5.6 %collective-permute-done.65 = bf16[896,128]{1,0:T(8,128)(2,1)S(1)} collective-permute-done((bf16[896,128]{1,0:T(8,128)(2,1)S(1)}, bf16[896,128]{1,0:T(8,128)(2,1)S(1)}, u32[]{:S(2)}, u32[]{:S(2)}) %collective-permute-start.65) | collective-permute-done | bytes 229408 | tf_op jit(solution)/shard_map/ppermute | solution.py:547
  487.7 6.3 %concatenate.156 = bf16[1576,192]{1,0:T(8,128)(2,1)S(1)} concatenate(bf16[197,192]{1,0:T(8,128)(2,1)} %get-tuple-element.214, bf16[197,192]{1,0:T(8,128)(2,1)} %get-tuple-element.213, bf16[197,192]{1,0:T(8,128)(2,1)} %get-tuple-element.212, bf16[197,192]{1,0:T(8,128)(2,1)} %get-tuple-element.211, bf16[197,192]{1,0:T(8,128)(2,1)} %get-tuple-element.210, ...), dimensions={0} | concatenate | bytes 1210368 | tf_op jit(solution)/shard_map/concatenate | solution.py:647
  (411 shorter events, 142.4 us)
Async XLA Ops:
  5.2 19.9 %collective-permute-start.13 = (bf16[264,384]{1,0:T(8,128)(2,1)}, bf16[264,384]{1,0:T(8,128)(2,1)}, u32[]{:S(2)}, u32[]{:S(2)}) collective-permute-start(bf16[264,384]{1,0:T(8,128)(2,1)} %pad_maximum_fusion.18), channel_id=1, source_target_pairs={{0,3},{1,2},{2,1},{3,0},{4,7},{5,6},{6,5},{7,4},{8,11},{9,10},{10,... | collective-permute-start | bytes 608264 | tf_op jit(solution)/shard_map/ppermute | solution.py:547
  9.1 16.4 %collective-permute-start.14 = (bf16[264,384]{1,0:T(8,128)(2,1)}, bf16[264,384]{1,0:T(8,128)(2,1)}, u32[]{:S(2)}, u32[]{:S(2)}) collective-permute-start(bf16[264,384]{1,0:T(8,128)(2,1)} %pad_maximum_fusion.18), channel_id=1, source_target_pairs={{0,2},{1,3},{2,0},{3,1},{4,6},{5,7},{6,4},{7,5},{8,10},{9,11},{10,... | collective-permute-start | bytes 608264 | tf_op jit(solution)/shard_map/ppermute | solution.py:547
  9.6 17.7 %collective-permute-start.15 = (bf16[264,384]{1,0:T(8,128)(2,1)}, bf16[264,384]{1,0:T(8,128)(2,1)}, u32[]{:S(2)}, u32[]{:S(2)}) collective-permute-start(bf16[264,384]{1,0:T(8,128)(2,1)} %pad_maximum_fusion.18), channel_id=1, source_target_pairs={{0,1},{1,0},{2,3},{3,2},{4,5},{5,4},{6,7},{7,6},{8,9},{9,8},{10,11... | collective-permute-start | bytes 608264 | tf_op jit(solution)/shard_map/ppermute | solution.py:547
  21.9 30.0 %collective-permute-start.18 = (bf16[416,384]{1,0:T(8,128)(2,1)S(1)}, bf16[416,384]{1,0:T(8,128)(2,1)S(1)}, u32[]{:S(2)}, u32[]{:S(2)}) collective-permute-start(bf16[416,384]{1,0:T(8,128)(2,1)S(1)} %get-tuple-element.119), channel_id=1, source_target_pairs={{0,3},{1,2},{2,1},{3,0},{4,7},{5,6},{6,5},{7,4},{8,11},{9,10},{10,... | collective-permute-start | bytes 958472 | tf_op jit(solution)/shard_map/ppermute | solution.py:547
  23.6 28.3 %collective-permute-start.19 = (bf16[416,384]{1,0:T(8,128)(2,1)S(1)}, bf16[416,384]{1,0:T(8,128)(2,1)S(1)}, u32[]{:S(2)}, u32[]{:S(2)}) collective-permute-start(bf16[416,384]{1,0:T(8,128)(2,1)S(1)} %get-tuple-element.120), channel_id=1, source_target_pairs={{0,2},{1,3},{2,0},{3,1},{4,6},{5,7},{6,4},{7,5},{8,10},{9,11},{10,... | collective-permute-start | bytes 958472 | tf_op jit(solution)/shard_map/ppermute | solution.py:547
  25.1 27.3 %collective-permute-start.20 = (bf16[416,384]{1,0:T(8,128)(2,1)S(1)}, bf16[416,384]{1,0:T(8,128)(2,1)S(1)}, u32[]{:S(2)}, u32[]{:S(2)}) collective-permute-start(bf16[416,384]{1,0:T(8,128)(2,1)S(1)} %get-tuple-element.118), channel_id=1, source_target_pairs={{0,1},{1,0},{2,3},{3,2},{4,5},{5,4},{6,7},{7,6},{8,9},{9,8},{10,11... | collective-permute-start | bytes 958472 | tf_op jit(solution)/shard_map/ppermute | solution.py:547
  25.5 27.5 %collective-permute-start.1 = (bf16[3,192,384]{2,1,0:T(8,128)(2,1)S(1)}, bf16[3,192,384]{2,1,0:T(8,128)(2,1)S(1)}, u32[]{:S(2)}, u32[]{:S(2)}) collective-permute-start(bf16[3,192,384]{2,1,0:T(8,128)(2,1)S(1)} %copy-done.12), channel_id=1, source_target_pairs={{0,2},{1,3},{2,0},{3,1},{4,6},{5,7},{6,4},{7,5},{8,10},{9,11},{10,... | collective-permute-start | bytes 1327112 | tf_op jit(solution)/shard_map/ppermute | solution.py:547
  51.9 19.7 %collective-permute-start.4 = (bf16[3,192,384]{2,1,0:T(8,128)(2,1)S(1)}, bf16[3,192,384]{2,1,0:T(8,128)(2,1)S(1)}, u32[]{:S(2)}, u32[]{:S(2)}) collective-permute-start(bf16[3,192,384]{2,1,0:T(8,128)(2,1)S(1)} %copy-done.12), channel_id=1, source_target_pairs={{0,4},{4,0},{1,5},{5,1},{2,6},{6,2},{3,7},{7,3},{8,12},{12,8},{9,1... | collective-permute-start | bytes 1327112 | tf_op jit(solution)/shard_map/ppermute | solution.py:543
  52.0 17.9 %collective-permute-start.12 = (bf16[3,128,384]{2,1,0:T(8,128)(2,1)S(1)}, bf16[3,128,384]{2,1,0:T(8,128)(2,1)S(1)}, u32[]{:S(2)}, u32[]{:S(2)}) collective-permute-start(bf16[3,128,384]{2,1,0:T(8,128)(2,1)S(1)} %copy-done.17), channel_id=1, source_target_pairs={{0,4},{4,0},{1,5},{5,1},{2,6},{6,2},{3,7},{7,3},{8,12},{12,8},{9,1... | collective-permute-start | bytes 884744 | tf_op jit(solution)/shard_map/ppermute | solution.py:543
  52.4 16.8 %collective-permute-start.17 = (bf16[384,128]{1,0:T(8,128)(2,1)S(1)}, bf16[384,128]{1,0:T(8,128)(2,1)S(1)}, u32[]{:S(2)}, u32[]{:S(2)}) collective-permute-start(bf16[384,128]{1,0:T(8,128)(2,1)S(1)} %copy-done.20), channel_id=1, source_target_pairs={{0,4},{4,0},{1,5},{5,1},{2,6},{6,2},{3,7},{7,3},{8,12},{12,8},{9,1... | collective-permute-start | bytes 294920 | tf_op jit(solution)/shard_map/ppermute | solution.py:543
  53.0 13.9 %collective-permute-start.2 = (bf16[3,96,384]{2,1,0:T(8,128)(2,1)S(1)}, bf16[3,96,384]{2,1,0:T(8,128)(2,1)S(1)}, u32[]{:S(2)}, u32[]{:S(2)}) collective-permute-start(bf16[3,96,384]{2,1,0:T(8,128)(2,1)S(1)} %slice.445), channel_id=1, source_target_pairs={{0,1},{1,0},{2,3},{3,2},{4,5},{5,4},{6,7},{7,6},{8,9},{9,8},{10,11... | collective-permute-start | bytes 663560 | tf_op jit(solution)/shard_map/ppermute | solution.py:547
  71.6 19.4 %collective-permute-start.31 = (bf16[416,768]{1,0:T(8,128)(2,1)S(1)}, bf16[416,768]{1,0:T(8,128)(2,1)}, u32[]{:S(2)}, u32[]{:S(2)}) collective-permute-start(bf16[416,768]{1,0:T(8,128)(2,1)S(1)} %pad_maximum_fusion.6.refs_13_.refs_29_), channel_id=1, source_target_pairs={{0,2},{1,3},{2,0},{3,1},{4,6},{5,7},{6,4},{7,5},{8,10},{9,11},{10,... | collective-permute-start | bytes 1916936 | tf_op jit(solution)/shard_map/ppermute | solution.py:547
  73.3 20.2 %collective-permute-start.30 = (bf16[416,768]{1,0:T(8,128)(2,1)S(1)}, bf16[416,768]{1,0:T(8,128)(2,1)}, u32[]{:S(2)}, u32[]{:S(2)}) collective-permute-start(bf16[416,768]{1,0:T(8,128)(2,1)S(1)} %pad_maximum_fusion.6.refs_13_.refs_29_), channel_id=1, source_target_pairs={{0,1},{1,0},{2,3},{3,2},{4,5},{5,4},{6,7},{7,6},{8,9},{9,8},{10,11... | collective-permute-start | bytes 1916936 | tf_op jit(solution)/shard_map/ppermute | solution.py:547
  89.0 25.0 %collective-permute-start.22 = (bf16[416,768]{1,0:T(8,128)(2,1)}, bf16[416,768]{1,0:T(8,128)(2,1)S(1)}, u32[]{:S(2)}, u32[]{:S(2)}) collective-permute-start(bf16[416,768]{1,0:T(8,128)(2,1)} %get-tuple-element.31.refs_3_.refs_22_), channel_id=1, source_target_pairs={{0,2},{1,3},{2,0},{3,1},{4,6},{5,7},{6,4},{7,5},{8,10},{9,11},{10,... | collective-permute-start | bytes 1916936 | tf_op jit(solution)/shard_map/ppermute | solution.py:547
  90.4 23.6 %collective-permute-start.21 = (bf16[416,768]{1,0:T(8,128)(2,1)}, bf16[416,768]{1,0:T(8,128)(2,1)S(1)}, u32[]{:S(2)}, u32[]{:S(2)}) collective-permute-start(bf16[416,768]{1,0:T(8,128)(2,1)} %get-tuple-element.31.refs_3_.refs_22_), channel_id=1, source_target_pairs={{0,1},{1,0},{2,3},{3,2},{4,5},{5,4},{6,7},{7,6},{8,9},{9,8},{10,11... | collective-permute-start | bytes 1916936 | tf_op jit(solution)/shard_map/ppermute | solution.py:547
  92.0 21.5 %collective-permute-start.32 = (bf16[208,768]{1,0:T(8,128)(2,1)S(1)}, bf16[208,768]{1,0:T(8,128)(2,1)}, u32[]{:S(2)}, u32[]{:S(2)}) collective-permute-start(bf16[208,768]{1,0:T(8,128)(2,1)S(1)} %slice.471), channel_id=1, source_target_pairs={{0,1},{1,0},{2,3},{3,2},{4,5},{5,4},{6,7},{7,6},{8,9},{9,8},{10,11... | collective-permute-start | bytes 958472 | tf_op jit(solution)/shard_map/ppermute | solution.py:547
  94.5 19.0 %collective-permute-start.33 = (bf16[208,768]{1,0:T(8,128)(2,1)S(1)}, bf16[208,768]{1,0:T(8,128)(2,1)}, u32[]{:S(2)}, u32[]{:S(2)}) collective-permute-start(bf16[208,768]{1,0:T(8,128)(2,1)S(1)} %slice.472), channel_id=1, source_target_pairs={{0,2},{1,3},{2,0},{3,1},{4,6},{5,7},{6,4},{7,5},{8,10},{9,11},{10,... | collective-permute-start | bytes 958472 | tf_op jit(solution)/shard_map/ppermute | solution.py:547
  95.2 30.3 %collective-permute-start.34 = (bf16[416,768]{1,0:T(8,128)(2,1)S(1)}, bf16[416,768]{1,0:T(8,128)(2,1)}, u32[]{:S(2)}, u32[]{:S(2)}) collective-permute-start(bf16[416,768]{1,0:T(8,128)(2,1)S(1)} %pad_maximum_fusion.6.refs_13_.refs_29_), channel_id=1, source_target_pairs={{0,4},{4,0},{1,5},{5,1},{2,6},{6,2},{3,7},{7,3},{8,12},{12,8},{9,1... | collective-permute-start | bytes 1916936 | tf_op jit(solution)/shard_map/ppermute | solution.py:543
  114.0 13.9 %collective-permute-start.37 = (bf16[208,768]{1,0:T(8,128)(2,1)}, bf16[208,768]{1,0:T(8,128)(2,1)}, u32[]{:S(2)}, u32[]{:S(2)}) collective-permute-start(bf16[208,768]{1,0:T(8,128)(2,1)} %collective-permute-done.32.refs_16_), channel_id=1, source_target_pairs={{0,4},{4,0},{1,5},{5,1},{2,6},{6,2},{3,7},{7,3},{8,12},{12,8},{9,1... | collective-permute-start | bytes 958472 | tf_op jit(solution)/shard_map/ppermute | solution.py:543
  299.3 38.4 %collective-permute-start.39 = (bf16[1664,768]{1,0:T(8,128)(2,1)}, bf16[1664,768]{1,0:T(8,128)(2,1)}, u32[]{:S(2)}, u32[]{:S(2)}) collective-permute-start(bf16[1664,768]{1,0:T(8,128)(2,1)} %slice.365), channel_id=1, source_target_pairs={{0,4},{4,0},{1,5},{5,1},{2,6},{6,2},{3,7},{7,3},{8,12},{12,8},{9,1... | collective-permute-start | bytes 7667720 | tf_op jit(solution)/shard_map/ppermute | solution.py:543
  317.0 26.3 %collective-permute-start.47 = (bf16[1664,896]{1,0:T(8,128)(2,1)}, bf16[1664,896]{1,0:T(8,128)(2,1)}, u32[]{:S(2)}, u32[]{:S(2)}) collective-permute-start(bf16[1664,896]{1,0:T(8,128)(2,1)} %slice.399), channel_id=1, source_target_pairs={{0,4},{4,0},{1,5},{5,1},{2,6},{6,2},{3,7},{7,3},{8,12},{12,8},{9,1... | collective-permute-start | bytes 8945672 | tf_op jit(solution)/shard_map/ppermute | solution.py:543
  341.1 16.8 %collective-permute-start.41 = (bf16[2,208,768]{2,1,0:T(8,128)(2,1)S(1)}, bf16[2,208,768]{2,1,0:T(8,128)(2,1)S(1)}, u32[]{:S(2)}, u32[]{:S(2)}) collective-permute-start(bf16[2,208,768]{2,1,0:T(8,128)(2,1)S(1)} %pad_maximum_fusion.8), channel_id=1, source_target_pairs={{0,2},{1,3},{2,0},{3,1},{4,6},{5,7},{6,4},{7,5},{8,10},{9,11},{10,... | collective-permute-start | bytes 1916936 | tf_op jit(solution)/shard_map/ppermute | solution.py:547
  342.1 16.6 %collective-permute-start.40 = (bf16[2,208,768]{2,1,0:T(8,128)(2,1)S(1)}, bf16[2,208,768]{2,1,0:T(8,128)(2,1)S(1)}, u32[]{:S(2)}, u32[]{:S(2)}) collective-permute-start(bf16[2,208,768]{2,1,0:T(8,128)(2,1)S(1)} %pad_maximum_fusion.7), channel_id=1, source_target_pairs={{0,1},{1,0},{2,3},{3,2},{4,5},{5,4},{6,7},{7,6},{8,9},{9,8},{10,11... | collective-permute-start | bytes 1916936 | tf_op jit(solution)/shard_map/ppermute | solution.py:547
  361.3 30.7 %collective-permute-start.49 = (bf16[2,208,896]{2,1,0:T(8,128)(2,1)S(1)}, bf16[2,208,896]{2,1,0:T(8,128)(2,1)S(1)}, u32[]{:S(2)}, u32[]{:S(2)}) collective-permute-start(bf16[2,208,896]{2,1,0:T(8,128)(2,1)S(1)} %pad_maximum_fusion.2), channel_id=1, source_target_pairs={{0,2},{1,3},{2,0},{3,1},{4,6},{5,7},{6,4},{7,5},{8,10},{9,11},{10,... | collective-permute-start | bytes 2236424 | tf_op jit(solution)/shard_map/ppermute | solution.py:547
  362.6 29.5 %collective-permute-start.48 = (bf16[2,208,896]{2,1,0:T(8,128)(2,1)S(1)}, bf16[2,208,896]{2,1,0:T(8,128)(2,1)S(1)}, u32[]{:S(2)}, u32[]{:S(2)}) collective-permute-start(bf16[2,208,896]{2,1,0:T(8,128)(2,1)S(1)} %pad_maximum_fusion.1), channel_id=1, source_target_pairs={{0,1},{1,0},{2,3},{3,2},{4,5},{5,4},{6,7},{7,6},{8,9},{9,8},{10,11... | collective-permute-start | bytes 2236424 | tf_op jit(solution)/shard_map/ppermute | solution.py:547
  371.3 19.0 %collective-permute-start.44 = (bf16[208,384]{1,0:T(8,128)(2,1)S(1)}, bf16[208,384]{1,0:T(8,128)(2,1)S(1)}, u32[]{:S(2)}, u32[]{:S(2)}) collective-permute-start(bf16[208,384]{1,0:T(8,128)(2,1)S(1)} %pad_maximum_fusion.23), channel_id=1, source_target_pairs={{0,3},{1,2},{2,1},{3,0},{4,7},{5,6},{6,5},{7,4},{8,11},{9,10},{10,... | collective-permute-start | bytes 479240 | tf_op jit(solution)/shard_map/ppermute | solution.py:547
  372.9 17.8 %collective-permute-start.45 = (bf16[208,384]{1,0:T(8,128)(2,1)S(1)}, bf16[208,384]{1,0:T(8,128)(2,1)S(1)}, u32[]{:S(2)}, u32[]{:S(2)}) collective-permute-start(bf16[208,384]{1,0:T(8,128)(2,1)S(1)} %pad_maximum_fusion.24), channel_id=1, source_target_pairs={{0,2},{1,3},{2,0},{3,1},{4,6},{5,7},{6,4},{7,5},{8,10},{9,11},{10,... | collective-permute-start | bytes 479240 | tf_op jit(solution)/shard_map/ppermute | solution.py:547
  374.0 17.6 %collective-permute-start.46 = (bf16[208,384]{1,0:T(8,128)(2,1)S(1)}, bf16[208,384]{1,0:T(8,128)(2,1)S(1)}, u32[]{:S(2)}, u32[]{:S(2)}) collective-permute-start(bf16[208,384]{1,0:T(8,128)(2,1)S(1)} %pad_maximum_fusion.25), channel_id=1, source_target_pairs={{0,1},{1,0},{2,3},{3,2},{4,5},{5,4},{6,7},{7,6},{8,9},{9,8},{10,11... | collective-permute-start | bytes 479240 | tf_op jit(solution)/shard_map/ppermute | solution.py:547
  433.2 39.6 %collective-permute-start.52 = (bf16[208,384]{1,0:T(8,128)(2,1)S(1)}, bf16[208,384]{1,0:T(8,128)(2,1)S(1)}, u32[]{:S(2)}, u32[]{:S(2)}) collective-permute-start(bf16[208,384]{1,0:T(8,128)(2,1)S(1)} %pad_maximum_fusion.27), channel_id=1, source_target_pairs={{0,3},{1,2},{2,1},{3,0},{4,7},{5,6},{6,5},{7,4},{8,11},{9,10},{10,... | collective-permute-start | bytes 479240 | tf_op jit(solution)/shard_map/ppermute | solution.py:547
  434.9 38.8 %collective-permute-start.53 = (bf16[208,384]{1,0:T(8,128)(2,1)S(1)}, bf16[208,384]{1,0:T(8,128)(2,1)S(1)}, u32[]{:S(2)}, u32[]{:S(2)}) collective-permute-start(bf16[208,384]{1,0:T(8,128)(2,1)S(1)} %pad_maximum_fusion.28), channel_id=1, source_target_pairs={{0,2},{1,3},{2,0},{3,1},{4,6},{5,7},{6,4},{7,5},{8,10},{9,11},{10,... | collective-permute-start | bytes 479240 | tf_op jit(solution)/shard_map/ppermute | solution.py:547
  437.3 16.6 %collective-permute-start.57 = (bf16[896,128]{1,0:T(8,128)(2,1)S(1)}, bf16[896,128]{1,0:T(8,128)(2,1)S(1)}, u32[]{:S(2)}, u32[]{:S(2)}) collective-permute-start(bf16[896,128]{1,0:T(8,128)(2,1)S(1)} %get-tuple-element.128), channel_id=1, source_target_pairs={{0,2},{1,3},{2,0},{3,1},{4,6},{5,7},{6,4},{7,5},{8,10},{9,11},{10,... | collective-permute-start | bytes 688136 | tf_op jit(solution)/shard_map/ppermute | solution.py:547
  438.5 15.4 %collective-permute-start.58 = (bf16[896,128]{1,0:T(8,128)(2,1)S(1)}, bf16[896,128]{1,0:T(8,128)(2,1)S(1)}, u32[]{:S(2)}, u32[]{:S(2)}) collective-permute-start(bf16[896,128]{1,0:T(8,128)(2,1)S(1)} %get-tuple-element.127), channel_id=1, source_target_pairs={{0,3},{1,2},{2,1},{3,0},{4,7},{5,6},{6,5},{7,4},{8,11},{9,10},{10,... | collective-permute-start | bytes 688136 | tf_op jit(solution)/shard_map/ppermute | solution.py:547
  (102 other events, 1200.7 us)
